TPU v7x, 32 devices: a whole 2x2x4 slice. The times are simulated.
32 devices in a mesh: row: 4 (over z), col: 8 (over y, x, core).
Axes of the slice: x: 2, y: 2, z: 4, core: 2. Of those that a mesh axis runs over, the one named last changes fastest.
Arguments:
- positions: float32 [1024, 24576], P('row', 'col'), may hold values from -2.5 to 2.5
- momenta: float32 [1024, 24576], P('row', 'col'), may hold values from -2.5 to 2.5
- couplings: float32 [24576, 24576], P('row', 'col'), may hold values from -0.0390625 to 0.0390625
Outputs:
- positions_next: float32 [1024, 24576], P('row', 'col')
- momenta_next: float32 [1024, 24576], P('row', 'col')
All inputs are finite; a program needn't handle non-finite values.
Results may differ from a plain program's by a relative error of at most 0.00005.
Values sent between devices are 32-bit elements; how exact they have to be, the bound alone decides.
No kernel may reach another device: no remote copies, remote signals or barrier semaphores. Data moves between devices by JAX's collectives and lax.ppermute only.
A program may use at most 192 MiB of HBM per device.

v0:
```python
import jax
import jax.numpy as jnp
from jax import lax
from jax.sharding import PartitionSpec as P

time_step = 0.5
kerr_rate = 1.0
pump_rate = 0.6
detuning = 0.4
coupling_gain = 1.5


def from_root(x, axis, root):
    mine = lax.axis_index(axis) == root
    return lax.psum(jnp.where(mine, x, jnp.zeros_like(x)), axis)


def column_blocks(positions):
    return lax.all_gather(positions, "row", axis=0, tiled=True)


def per_device(positions, momenta, couplings):
    row_index = lax.axis_index("row")
    root_col = 2 * row_index
    column_block = column_blocks(positions)
    first_half = from_root(column_block, "col", root_col)
    second_half = from_root(column_block, "col", root_col + 1)
    gathered = jnp.concatenate([first_half, second_half], axis=1)
    partial_force = jnp.dot(
        gathered, couplings, precision=lax.Precision.HIGHEST, preferred_element_type=jnp.float32
    )
    coupled = lax.psum_scatter(partial_force, "row", scatter_dimension=0, tiled=True)
    radius = positions * positions + momenta * momenta
    momenta_next = momenta + time_step * (
        -(kerr_rate * radius - pump_rate + detuning) * positions + coupling_gain * coupled
    )
    radius_next = positions * positions + momenta_next * momenta_next
    positions_next = (
        positions + time_step * (kerr_rate * radius_next + pump_rate + detuning) * momenta_next
    )
    return (positions_next, momenta_next)


def solution(mesh):
    placed = (P("row", "col"), P("row", "col"), P("row", "col"))
    return jax.shard_map(
        per_device,
        mesh=mesh,
        in_specs=placed,
        out_specs=(P("row", "col"), P("row", "col")),
        check_vma=False,
    )
```

profile of v0, /device:TPU:0, one launch (start us, length us, event | category | flops | bytes accessed | tf_op | source)
XLA Modules:
  0.0 1026.9 jit_solution(14920219728477134093)
XLA Ops:
  7.2 0.0 all-gather.2.cloned.1.call-start
  7.2 0.7 all-gather.2.cloned.1.call-update
  7.9 0.0 all-reduce.3.cloned.1.call-start
  8.0 222.6 %all-gather.2.cloned.1.call-done = f32[1024,3072]{1,0:T(8,128)} async-done(((f32[256,3072]{1,0:T(8,128)}), f32[1024,3072]{1,0:T(8,128)}) %all-gather.2.cloned.1.call-update) | async-done | bytes 12582928 | tf_op jit(solution)/shard_map/all_gather | solution.py:19
  230.5 13.7 %broadcast_select_fusion.1 = (f32[1024,3072]{1,0:T(8,128)}, f32[1024,3072]{1,0:T(8,128)}) fusion(f32[1024,3072]{1,0:T(8,128)} %all-gather.2.cloned.1.call-done, pred[]{:T(512)S(6)} %eq.6, pred[]{:T(512)S(6)} %eq.7), kind=kLoop, calls=%fused_computation.5 | loop fusion | flops 6291456 | bytes 37748736 | tf_op jit(solution)/shard_map/jit(_where)/select_n | solution.py:15
  244.2 0.0 all-reduce.3.cloned.1.call-update
  244.2 0.0 reduce-scatter.2.cloned.1.call-start
  244.3 306.1 %all-reduce.3.cloned.1.call-done = (f32[1024,3072]{1,0:T(8,128)}, f32[1024,3072]{1,0:T(8,128)}) async-done(((f32[1024,3072]{1,0:T(8,128)}, f32[1024,3072]{1,0:T(8,128)}), (f32[1024,3072]{1,0:T(8,128)}, f32[1024,3072]{1,0:T(8,128)})) %all-reduce.3.cloned.1.call-update) | async-done | bytes 25165840 | tf_op jit(solution)/shard_map/psum | solution.py:15
  550.4 250.7 %fusion = f32[1024,3072]{1,0:T(8,128)} fusion(f32[6144,3072]{1,0:T(8,128)} %param.5, f32[1024,3072]{1,0:T(8,128)} %get-tuple-element.2, f32[1024,3072]{1,0:T(8,128)} %get-tuple-element.3), kind=kOutput, calls=%fused_computation | convolution fusion | flops 231934525440 | bytes 113246208 | tf_op jit(solution)/shard_map/dot_general | solution.py:29
  801.1 0.0 copy-start
  801.1 0.0 reduce-scatter.2.cloned.1.call-update
  801.1 212.1 %reduce-scatter.2.cloned.1.call-done = f32[256,3072]{1,0:T(8,128)} async-done(((f32[1024,3072]{1,0:T(8,128)}), f32[256,3072]{1,0:T(8,128)}) %reduce-scatter.2.cloned.1.call-update) | async-done | bytes 3145744 | tf_op jit(solution)/shard_map/reduce_scatter | solution.py:32
  1013.2 0.0 copy-done
  1013.2 7.2 multiply_add_fusion
Async XLA Ops:
  7.2 223.3 %all-gather.2.cloned.1.call-start = ((), (), s32[]{:S(2)}) async-start(), calls=%async_computation.1 | async-start | bytes 15728640 | tf_op jit(solution)/shard_map/all_gather | solution.py:19
  7.9 542.5 %all-reduce.3.cloned.1.call-start = ((), (), s32[]{:S(2)}) async-start(), calls=%async_computation.3 | async-start | bytes 50331648 | tf_op jit(solution)/shard_map/psum | solution.py:15
  244.2 769.0 %reduce-scatter.2.cloned.1.call-start = ((), (), s32[]{:S(2)}) async-start(), calls=%async_computation.2 | async-start | bytes 15728640 | tf_op jit(solution)/shard_map/reduce_scatter | solution.py:32
  801.1 212.1 %copy-start = (f32[256,3072]{1,0:T(8,128)S(1)}, f32[256,3072]{1,0:T(8,128)}, u32[]{:S(2)}) copy-start(f32[256,3072]{1,0:T(8,128)} %param.3) | copy-start | bytes 9437188
Sparse Core Ops, SparseCore 0:
  9.6 220.8 all-gather.1
  244.4 305.9 all-reduce.2
  801.2 211.9 reduce-scatter.1
where the time goes:
time: 1030 us
  waiting for transfers between devices  741 us (72%)
  matrix products  251 us (24%)
  other arithmetic  20.9 us (2%)
  between operations  13.8 us (1%)
    psum x1, waiting for transfers between devices, from_root(): return lax.psum(jnp.where(mine, x, jnp.zeros_like(x)), axis)  306 us
    dot_general x1, matrix products, per_device(): jnp.dot(gathered, couplings, precision=lax.Precision.HIGHEST, preferred_e...  251 us
    all_gather x1, waiting for transfers between devices, column_blocks(): return lax.all_gather(positions, 'row', axis=0, tiled=True)  223 us
    reduce_scatter x1, waiting for transfers between devices, per_device(): lax.psum_scatter(partial_force, 'row', scatter_dimension=0, tiled=True)  212 us
  transfers between devices with their start and end apart: 3, of which 3 were waited for; matrix products, arithmetic and copies ran while one was open for 0% of the time, Pallas kernels for 0%

commit v1 on v0

v1 whole, which is shorter than its diff:
```python
import functools

import jax
import jax.numpy as jnp
from jax import lax
from jax.experimental import pallas as pl
from jax.experimental.pallas import tpu as pltpu
from jax.sharding import PartitionSpec as P

time_step = 0.5
kerr_rate = 1.0
pump_rate = 0.6
detuning = 0.4
coupling_gain = 1.5

CHUNKS = 3
VMEM = 56 * 2**20
f32, bf16 = jnp.float32, jnp.bfloat16


def halves(x):
    high = x.astype(bf16)
    return high, (x - high.astype(f32)).astype(bf16)


def products(split_ref, c_ref, o_ref, depth):
    k = pl.program_id(1)
    columns = pl.ds(pl.multiple_of(k * depth, depth), depth)
    high, low = halves(c_ref[...])
    p_high = split_ref[0, :, columns]
    part = jnp.dot(p_high, high, preferred_element_type=f32)
    part += jnp.dot(split_ref[1, :, columns], high, preferred_element_type=f32)
    part += jnp.dot(p_high, low, preferred_element_type=f32)

    @pl.when(k == 0)
    def _():
        o_ref[...] = part

    @pl.when(k > 0)
    def _():
        o_ref[...] += part


def first_kernel(p_ref, c_ref, o_ref, split_ref):
    sites, _, rows, depth = p_ref.shape
    k = pl.program_id(1)

    @pl.when(pl.program_id(0) == 0)
    def _():
        columns = pl.ds(pl.multiple_of(k * depth, depth), depth)
        for j in range(sites):
            high, low = halves(p_ref[j, k])
            split_ref[0, pl.ds(j * rows, rows), columns] = high
            split_ref[1, pl.ds(j * rows, rows), columns] = low

    products(split_ref, c_ref, o_ref, depth)


def next_kernel(split_ref, c_ref, o_ref):
    products(split_ref, c_ref, o_ref, c_ref.shape[0])


def block_product(block, couplings, parts, start, width):
    depth = couplings.shape[0] // parts
    first = block.ndim == 4
    rows = block.shape[0] * block.shape[2] if first else block.shape[1]
    split = jax.ShapeDtypeStruct((2, rows, depth * parts), bf16)
    tile = min(512, width)
    whole = pl.BlockSpec(block.shape, lambda i, k: (0,) * block.ndim, pipeline_mode=pl.Buffered(1))
    out_shape = [jax.ShapeDtypeStruct((rows, width), f32)]
    out_specs = [pl.BlockSpec((rows, tile), lambda i, k: (0, i))]
    if first:
        out_shape.append(split)
        out_specs.append(pl.BlockSpec(split.shape, lambda i, k: (0, 0, 0)))
    out = pl.pallas_call(
        first_kernel if first else next_kernel,
        grid=(width // tile, parts),
        in_specs=[whole, pl.BlockSpec((depth, tile), lambda i, k: (k, start // tile + i))],
        out_specs=out_specs,
        out_shape=out_shape,
        compiler_params=pltpu.CompilerParams(vmem_limit_bytes=VMEM),
        cost_estimate=pl.CostEstimate(flops=0, bytes_accessed=2**20, transcendentals=0),
    )(block, couplings)
    return out[0], (out[1] if first else block)


def after(x, *others):
    return lax.optimization_barrier((x, *others))[0]


class Plan:
    def __init__(self, n, cols):
        self.n, self.cols, self.ratio = n, cols, cols // n
        assert self.ratio * n == cols
        self.order = [[self.shift(z, a) for a in range(n - 1, -1, -1)] for z in range(n)]
        self.slot = [[self.order[z].index(s) for s in range(n)] for z in range(n)]

    def shift(self, a, b):
        return a ^ b if self.n & (self.n - 1) == 0 else (a + b) % self.n

    def unshift(self, a, b):
        return a ^ b if self.n & (self.n - 1) == 0 else (a - b) % self.n

    def site_pairs(self, m):
        r = self.ratio
        return [(q * r + c, self.shift(q, m) * r + c) for q in range(self.n) for c in range(r)]


def shift(plan, a, b):
    return a ^ b if plan.n & (plan.n - 1) == 0 else lax.rem(a + b, plan.n)


def unshift(plan, a, b):
    return a ^ b if plan.n & (plan.n - 1) == 0 else lax.rem(a - b + plan.n, plan.n)


def one_of(values, index):
    out = values[0]
    for i in range(1, len(values)):
        out = jnp.where(index == i, values[i], out)
    return out


def pick(values, choice, index):
    used = sorted({c for c in choice if c is not None})
    out = values[used[0]]
    for c in used[1:]:
        mine = functools.reduce(jnp.logical_or, [index == i for i, v in enumerate(choice) if v == c])
        out = jnp.where(mine, values[c], out)
    return out


def spread_sites(plan, positions, col):
    n = plan.n
    site = col // plan.ratio
    rows = positions.shape[0] // n
    arrived = []
    for m in range(n):
        j = shift(plan, site, m)
        part = lax.dynamic_slice_in_dim(positions, j * rows, rows, axis=0)
        arrived.append(part if m == 0 else lax.ppermute(part, "col", plan.site_pairs(m)))
    return [one_of(arrived, unshift(plan, site, q)) for q in range(n)]


def gather_slot(plan, k, spread, row):
    n = plan.n
    target = [[plan.order[z][k] for z in range(n)].index(r) for r in range(n)]
    part = pick(spread, target, row)
    pairs = [(r, target[r]) for r in range(n)]
    if any(a != b for a, b in pairs):
        part = lax.ppermute(part, "row", pairs)
    whole = lax.all_gather(part, "col", axis=0, tiled=False)
    return whole.reshape(n, plan.ratio, *part.shape)


def per_device(plan, positions, momenta, couplings):
    n = plan.n
    row, col = lax.axis_index("row"), lax.axis_index("col")
    width = positions.shape[1]
    chunk = width // CHUNKS
    lanes = [slice(c * chunk, (c + 1) * chunk) for c in range(CHUNKS)]

    spread = spread_sites(plan, positions, col)
    gathered = [gather_slot(plan, k, spread, row) for k in range(n)]

    partial = [[None] * CHUNKS for _ in range(n)]
    from_below, from_above = [None] * CHUNKS, [None] * CHUNKS
    last = None
    for k in range(n):
        block = gathered[k]
        for c in range(CHUNKS):
            if last is not None:
                block = after(block, last)
            last, block = block_product(block, couplings, plan.ratio, lanes[c].start, chunk)
            partial[k][c] = last
            t = k
            if t == n - 1:
                continue
            up = [plan.slot[z][n - 1 - t + z] if z <= t else None for z in range(n)]
            down = [plan.slot[z][z - (n - 1 - t)] if z >= n - 1 - t else None for z in range(n)]
            here = [partial[i][c] for i in range(n)]
            above, below = pick(here, up, row), pick(here, down, row)
            if t:
                above, below = above + from_below[c], below + from_above[c]
            from_below[c] = lax.ppermute(above, "row", [(z, z + 1) for z in range(t + 1)])
            from_above[c] = lax.ppermute(below, "row", [(z, z - 1) for z in range(n - 1 - t, n)])

    outs = []
    for c in range(CHUNKS):
        coupled = pick([partial[k][c] for k in range(n)], [plan.slot[z][z] for z in range(n)], row)
        if n > 1:
            coupled = coupled + from_below[c] + from_above[c]
        x, y = positions[:, lanes[c]], momenta[:, lanes[c]]
        radius = x * x + y * y
        y_next = y + time_step * (
            -(kerr_rate * radius - pump_rate + detuning) * x + coupling_gain * coupled
        )
        radius_next = x * x + y_next * y_next
        x_next = x + time_step * (kerr_rate * radius_next + pump_rate + detuning) * y_next
        outs.append((x_next, y_next))
    return (
        jnp.concatenate([o[0] for o in outs], axis=1),
        jnp.concatenate([o[1] for o in outs], axis=1),
    )


def solution(mesh):
    placed = (P("row", "col"), P("row", "col"), P("row", "col"))
    plan = Plan(mesh.shape["row"], mesh.shape["col"])

    def step(positions, momenta, couplings):
        return per_device(plan, positions, momenta, couplings)

    return jax.shard_map(
        step,
        mesh=mesh,
        in_specs=placed,
        out_specs=(P("row", "col"), P("row", "col")),
        check_vma=False,
    )
```

time: 1030 us -> 446 us (0.43)
  waiting for transfers between devices: 741 us -> 108 us
  matrix products: 251 us -> 0 us
  Pallas kernels: 0 us -> 212 us
  starting transfers between devices: 0.12 us -> 68.7 us
    psum x1 -> x0, waiting for transfers between devices: 306 us -> none  [from_root(): return lax.psum(jnp.where(mine, x, jnp.zeros_like(x)), axis)]
    dot_general x1 -> x0, matrix products: 251 us -> none  [per_device(): jnp.dot(gathered, couplings, precision=lax.Precision.HIGHEST, preferred_e...]
    all_gather x1 -> x4, waiting for transfers between devices: 223 us -> 0.08 us  [gather_slot(): whole = lax.all_gather(part, 'col', axis=0, tiled=False)]
    reduce_scatter x1 -> x0, waiting for transfers between devices: 212 us -> none  [per_device(): lax.psum_scatter(partial_force, 'row', scatter_dimension=0, tiled=True)]
    pallas_call x0 -> x12, Pallas kernels: none -> 212 us  [block_product(): pl.pallas_call(first_kernel if first else next_kernel, grid=(width // til...]
    ppermute x0 -> x24, waiting for transfers between devices: none -> 108 us  [the longest x3 69.6 us: gather_slot(): part = lax.ppermute(part, 'row', pairs)]
    ppermute x0 -> x24, starting transfers between devices: none -> 68.6 us  [the longest x9 29.7 us: per_device(): lax.ppermute(above, 'row', [(z, z + 1) for z in range(t + 1)])]
    add x1 -> x7, other arithmetic: 7.17 us -> 22.8 us  [the longest x6 18.4 us: per_device(): above, below = (above + from_below[c], below + from_above[c])]
  transfers between devices with their start and end apart: 3 -> 28, of which waited for: 3 -> 7; matrix products, arithmetic and copies ran while one was open for 0% -> 4% of each run, Pallas kernels for 0% -> 48%
where the time goes in v1:
time: 446 us; the launch traced here: 438 us
  Pallas kernels  212 us (48%)
  waiting for transfers between devices  108 us (24%)
  starting transfers between devices  68.7 us (15%)
  other arithmetic  28.9 us (6%)
  between operations  14.5 us (3%)
  local copies, waits for them, and re-layouts  5.38 us (1%)
    pallas_call x12, Pallas kernels, block_product(): pl.pallas_call(first_kernel if first else next_kernel, grid=(width // til...  212 us
    ppermute x3, waiting for transfers between devices, gather_slot(): part = lax.ppermute(part, 'row', pairs)  69.6 us
    ppermute x3, waiting for transfers between devices, spread_sites(): lax.ppermute(part, 'col', plan.site_pairs(m))  34.4 us
    ppermute x9, starting transfers between devices, per_device(): lax.ppermute(above, 'row', [(z, z + 1) for z in range(t + 1)])  29.7 us
    ppermute x3, starting transfers between devices, gather_slot(): part = lax.ppermute(part, 'row', pairs)  21.3 us
    add x6, other arithmetic, per_device(): above, below = (above + from_below[c], below + from_above[c])  18.4 us
    ppermute x9, starting transfers between devices, per_device(): lax.ppermute(below, 'row', [(z, z - 1) for z in range(n - 1 - t, n)])  13.1 us
  transfers between devices with their start and end apart: 28, of which 7 were waited for; matrix products, arithmetic and copies ran while one was open for 4% of the time, Pallas kernels for 48%

profile of v1, /device:TPU:0, one launch (start us, length us, event | category | flops | bytes accessed | tf_op | source)
XLA Modules:
  0.0 437.7 jit_solution(2087995467362386637)
XLA Ops:
  9.9 3.9 collective-permute-start
  14.4 18.1 %collective-permute-done = f32[64,3072]{1,0:T(8,128)S(1)} collective-permute-done((f32[64,3072]{1,0:T(8,128)}, f32[64,3072]{1,0:T(8,128)S(1)}, u32[]{:S(2)}, u32[]{:S(2)}) %collective-permute-start) | collective-permute-done | bytes 786464 | tf_op jit(solution)/shard_map/ppermute | solution.py:141
  32.4 16.0 %collective-permute-done.1 = f32[64,3072]{1,0:T(8,128)S(1)} collective-permute-done((f32[64,3072]{1,0:T(8,128)S(1)}, f32[64,3072]{1,0:T(8,128)S(1)}, u32[]{:S(2)}, u32[]{:S(2)}) %collective-permute-start.1) | collective-permute-done | bytes 786464 | tf_op jit(solution)/shard_map/ppermute | solution.py:141
  55.5 17.7 %collective-permute-done.5 = f32[64,3072]{1,0:T(8,128)S(1)} collective-permute-done((f32[64,3072]{1,0:T(8,128)S(1)}, f32[64,3072]{1,0:T(8,128)S(1)}, u32[]{:S(2)}, u32[]{:S(2)}) %collective-permute-start.5) | collective-permute-done | bytes 786464 | tf_op jit(solution)/shard_map/ppermute | solution.py:151
  74.2 17.5 %collective-permute-start.4 = (f32[64,3072]{1,0:T(8,128)S(1)}, f32[64,3072]{1,0:T(8,128)S(1)}, u32[]{:S(2)}, u32[]{:S(2)}) collective-permute-start(f32[64,3072]{1,0:T(8,128)S(1)} %get-tuple-element.56), channel_id=1, source_target_pairs={{0,16},{8,24},{16,0},{24,8},{1,17},{9,25},{17,1},{25,9},{2,18},{10... | collective-permute-start | bytes 2359304 | tf_op jit(solution)/shard_map/ppermute | solution.py:151
  91.8 33.6 %collective-permute-done.4 = f32[64,3072]{1,0:T(8,128)S(1)} collective-permute-done((f32[64,3072]{1,0:T(8,128)S(1)}, f32[64,3072]{1,0:T(8,128)S(1)}, u32[]{:S(2)}, u32[]{:S(2)}) %collective-permute-start.4) | collective-permute-done | bytes 786464 | tf_op jit(solution)/shard_map/ppermute | solution.py:151
  126.4 18.2 %collective-permute-done.3 = f32[64,3072]{1,0:T(8,128)S(1)} collective-permute-done((f32[64,3072]{1,0:T(8,128)S(1)}, f32[64,3072]{1,0:T(8,128)S(1)}, u32[]{:S(2)}, u32[]{:S(2)}) %collective-permute-start.3) | collective-permute-done | bytes 786464 | tf_op jit(solution)/shard_map/ppermute | solution.py:151
  146.2 19.4 %shard_map.50 = (f32[256,1024]{1,0:T(8,128)}, bf16[2,256,6144]{2,1,0:T(8,128)(2,1)}) custom-call(f32[4,2,64,3072]{3,2,1,0:T(8,128)} %bitcast.7, f32[6144,3072]{1,0:T(8,128)} %c_ref.23), custom_call_target="tpu_custom_call" | custom-call | bytes 1048576 | tf_op jit(solution)/shard_map/pallas_call | solution.py:75
  165.5 16.7 %shard_map.51 = f32[256,1024]{1,0:T(8,128)} custom-call(bf16[2,256,6144]{2,1,0:T(8,128)(2,1)} %get-tuple-element.24.split_ref, f32[6144,3072]{1,0:T(8,128)} %c_ref.23), custom_call_target="tpu_custom_call" | custom-call | bytes 1048576 | tf_op jit(solution)/shard_map/pallas_call | solution.py:75
  187.1 16.9 %shard_map.52 = f32[256,1024]{1,0:T(8,128)} custom-call(bf16[2,256,6144]{2,1,0:T(8,128)(2,1)} %get-tuple-element.24.split_ref, f32[6144,3072]{1,0:T(8,128)} %c_ref.23), custom_call_target="tpu_custom_call" | custom-call | bytes 1048576 | tf_op jit(solution)/shard_map/pallas_call | solution.py:75
  208.6 19.6 %shard_map.53 = (f32[256,1024]{1,0:T(8,128)}, bf16[2,256,6144]{2,1,0:T(8,128)(2,1)}) custom-call(f32[4,2,64,3072]{3,2,1,0:T(8,128)} %bitcast.6, f32[6144,3072]{1,0:T(8,128)} %c_ref.23), custom_call_target="tpu_custom_call" | custom-call | bytes 1048576 | tf_op jit(solution)/shard_map/pallas_call | solution.py:75
  228.2 16.9 %shard_map.54 = f32[256,1024]{1,0:T(8,128)} custom-call(bf16[2,256,6144]{2,1,0:T(8,128)(2,1)} %get-tuple-element.29.split_ref, f32[6144,3072]{1,0:T(8,128)} %c_ref.23), custom_call_target="tpu_custom_call" | custom-call | bytes 1048576 | tf_op jit(solution)/shard_map/pallas_call | solution.py:75
  253.9 17.5 %shard_map.55 = f32[256,1024]{1,0:T(8,128)} custom-call(bf16[2,256,6144]{2,1,0:T(8,128)(2,1)} %get-tuple-element.29.split_ref, f32[6144,3072]{1,0:T(8,128)} %c_ref.23), custom_call_target="tpu_custom_call" | custom-call | bytes 1048576 | tf_op jit(solution)/shard_map/pallas_call | solution.py:75
  278.8 19.3 %shard_map.56 = (f32[256,1024]{1,0:T(8,128)}, bf16[2,256,6144]{2,1,0:T(8,128)(2,1)}) custom-call(f32[4,2,64,3072]{3,2,1,0:T(8,128)} %bitcast.5, f32[6144,3072]{1,0:T(8,128)} %c_ref.23), custom_call_target="tpu_custom_call" | custom-call | bytes 1048576 | tf_op jit(solution)/shard_map/pallas_call | solution.py:75
  298.1 16.5 %shard_map.57 = f32[256,1024]{1,0:T(8,128)} custom-call(bf16[2,256,6144]{2,1,0:T(8,128)(2,1)} %get-tuple-element.34.split_ref, f32[6144,3072]{1,0:T(8,128)} %c_ref.23), custom_call_target="tpu_custom_call" | custom-call | bytes 1048576 | tf_op jit(solution)/shard_map/pallas_call | solution.py:75
  322.4 5.0 %collective-permute-start.14 = (f32[256,1024]{1,0:T(8,128)S(1)}, f32[256,1024]{1,0:T(8,128)}, u32[]{:S(2)}, u32[]{:S(2)}) collective-permute-start(f32[256,1024]{1,0:T(8,128)S(1)} %get-tuple-element.63), channel_id=1, source_target_pairs={{0,8},{8,16},{16,24},{1,9},{9,17},{17,25},{2,10},{10,18},{18,26},{... | collective-permute-start | bytes 3145736 | tf_op jit(solution)/shard_map/ppermute | solution.py:185
  327.4 16.4 %shard_map.58 = f32[256,1024]{1,0:T(8,128)} custom-call(bf16[2,256,6144]{2,1,0:T(8,128)(2,1)} %get-tuple-element.34.split_ref, f32[6144,3072]{1,0:T(8,128)} %c_ref.23), custom_call_target="tpu_custom_call" | custom-call | bytes 1048576 | tf_op jit(solution)/shard_map/pallas_call | solution.py:75
  345.2 3.8 select_add_fusion.1
  349.1 5.6 %collective-permute-start.20 = (f32[256,1024]{1,0:T(8,128)}, f32[256,1024]{1,0:T(8,128)}, u32[]{:S(2)}, u32[]{:S(2)}) collective-permute-start(f32[256,1024]{1,0:T(8,128)} %get-tuple-element.65), channel_id=1, source_target_pairs={{0,8},{8,16},{16,24},{1,9},{9,17},{17,25},{2,10},{10,18},{18,26},{... | collective-permute-start | bytes 3145736 | tf_op jit(solution)/shard_map/ppermute | solution.py:185
  364.4 6.1 %collective-permute-start.8 = (f32[256,1024]{1,0:T(8,128)}, f32[256,1024]{1,0:T(8,128)}, u32[]{:S(2)}, u32[]{:S(2)}) collective-permute-start(f32[256,1024]{1,0:T(8,128)} %get-tuple-element.61), channel_id=1, source_target_pairs={{0,8},{8,16},{16,24},{1,9},{9,17},{17,25},{2,10},{10,18},{18,26},{... | collective-permute-start | bytes 3145736 | tf_op jit(solution)/shard_map/ppermute | solution.py:185
  370.6 19.4 %shard_map.59 = (f32[256,1024]{1,0:T(8,128)}, bf16[2,256,6144]{2,1,0:T(8,128)(2,1)}) custom-call(f32[4,2,64,3072]{3,2,1,0:T(8,128)} %bitcast.4, f32[6144,3072]{1,0:T(8,128)} %c_ref.23), custom_call_target="tpu_custom_call" | custom-call | bytes 1048576 | tf_op jit(solution)/shard_map/pallas_call | solution.py:75
  390.0 16.5 %shard_map.60 = f32[256,1024]{1,0:T(8,128)} custom-call(bf16[2,256,6144]{2,1,0:T(8,128)(2,1)} %get-tuple-element.39.split_ref, f32[6144,3072]{1,0:T(8,128)} %c_ref.23), custom_call_target="tpu_custom_call" | custom-call | bytes 1048576 | tf_op jit(solution)/shard_map/pallas_call | solution.py:75
  406.5 16.7 %shard_map.61 = f32[256,1024]{1,0:T(8,128)} custom-call(bf16[2,256,6144]{2,1,0:T(8,128)(2,1)} %get-tuple-element.39.split_ref, f32[6144,3072]{1,0:T(8,128)} %c_ref.23), custom_call_target="tpu_custom_call" | custom-call | bytes 1048576 | tf_op jit(solution)/shard_map/pallas_call | solution.py:75
  423.2 4.4 %multiply_add_fusion.4 = (f32[256,1024]{1,0:T(8,128)S(1)}, f32[256,1024]{1,0:T(8,128)S(1)}, f32[256,1024]{1,0:T(8,128)S(1)}, f32[256,1024]{1,0:T(8,128)S(1)}, f3...) fusion(f32[256,3072]{1,0:T(8,128)S(1)} %copy-done, f32[256,1024]{1,0:T(8,128)} %collective-permute-done.11, ...), kind=kLoop, calls=%fused_computation.10 | loop fusion | flops 14155776 | bytes 22020096 | tf_op jit(solution)/shard_map/add | solution.py:199
  (83 shorter events, 61.5 us)
Async XLA Ops:
  7.2 139.0 %all-gather.15.cloned.1.call-start = ((), (), s32[]{:S(2)}) async-start(), calls=%async_computation.3 | async-start | bytes 7077888 | tf_op jit(solution)/shard_map/all_gather | solution.py:152
  13.8 34.6 %collective-permute-start.1 = (f32[64,3072]{1,0:T(8,128)S(1)}, f32[64,3072]{1,0:T(8,128)S(1)}, u32[]{:S(2)}, u32[]{:S(2)}) collective-permute-start(f32[64,3072]{1,0:T(8,128)S(1)} %get-tuple-element.59), channel_id=1, source_target_pairs={{0,4},{1,5},{2,6},{3,7},{4,0},{5,1},{6,2},{7,3},{8,12},{9,13},{10,... | collective-permute-start | bytes 2359304 | tf_op jit(solution)/shard_map/ppermute | solution.py:141
  74.2 134.5 %all-gather.13.cloned.1.call-start = ((), (), s32[]{:S(2)}) async-start(), calls=%async_computation.2 | async-start | bytes 7077888 | tf_op jit(solution)/shard_map/all_gather | solution.py:152
  74.2 51.2 %collective-permute-start.4 = (f32[64,3072]{1,0:T(8,128)S(1)}, f32[64,3072]{1,0:T(8,128)S(1)}, u32[]{:S(2)}, u32[]{:S(2)}) collective-permute-start(f32[64,3072]{1,0:T(8,128)S(1)} %get-tuple-element.56), channel_id=1, source_target_pairs={{0,16},{8,24},{16,0},{24,8},{1,17},{9,25},{17,1},{25,9},{2,18},{10... | collective-permute-start | bytes 2359304 | tf_op jit(solution)/shard_map/ppermute | solution.py:151
  126.3 152.5 %all-gather.11.cloned.1.call-start = ((), (), s32[]{:S(2)}) async-start(), calls=%async_computation.1 | async-start | bytes 7077888 | tf_op jit(solution)/shard_map/all_gather | solution.py:152
  145.6 225.0 %all-gather.9.cloned.1.call-start = ((), (), s32[]{:S(2)}) async-start(), calls=%async_computation | async-start | bytes 7077888 | tf_op jit(solution)/shard_map/all_gather | solution.py:152
  182.2 63.0 %collective-permute-start.12 = (f32[256,1024]{1,0:T(8,128)}, f32[256,1024]{1,0:T(8,128)}, u32[]{:S(2)}, u32[]{:S(2)}) collective-permute-start(f32[256,1024]{1,0:T(8,128)} %shard_map.51), channel_id=1, source_target_pairs={{0,8},{1,9},{2,10},{3,11},{4,12},{5,13},{6,14},{7,15}} | collective-permute-start | bytes 3145736 | tf_op jit(solution)/shard_map/ppermute | solution.py:185
  185.5 61.3 %collective-permute-start.15 = (f32[256,1024]{1,0:T(8,128)}, f32[256,1024]{1,0:T(8,128)}, u32[]{:S(2)}, u32[]{:S(2)}) collective-permute-start(f32[256,1024]{1,0:T(8,128)} %shard_map.51), channel_id=1, source_target_pairs={{24,16},{25,17},{26,18},{27,19},{28,20},{29,21},{30,22},{31,23}} | collective-permute-start | bytes 3145736 | tf_op jit(solution)/shard_map/ppermute | solution.py:186
  204.0 48.2 %collective-permute-start.18 = (f32[256,1024]{1,0:T(8,128)}, f32[256,1024]{1,0:T(8,128)S(1)}, u32[]{:S(2)}, u32[]{:S(2)}) collective-permute-start(f32[256,1024]{1,0:T(8,128)} %shard_map.52), channel_id=1, source_target_pairs={{0,8},{1,9},{2,10},{3,11},{4,12},{5,13},{6,14},{7,15}} | collective-permute-start | bytes 3145736 | tf_op jit(solution)/shard_map/ppermute | solution.py:185
  205.4 66.0 %collective-permute-start.21 = (f32[256,1024]{1,0:T(8,128)}, f32[256,1024]{1,0:T(8,128)}, u32[]{:S(2)}, u32[]{:S(2)}) collective-permute-start(f32[256,1024]{1,0:T(8,128)} %shard_map.52), channel_id=1, source_target_pairs={{24,16},{25,17},{26,18},{27,19},{28,20},{29,21},{30,22},{31,23}} | collective-permute-start | bytes 3145736 | tf_op jit(solution)/shard_map/ppermute | solution.py:186
  207.1 69.8 %collective-permute-start.6 = (f32[256,1024]{1,0:T(8,128)}, f32[256,1024]{1,0:T(8,128)S(1)}, u32[]{:S(2)}, u32[]{:S(2)}) collective-permute-start(f32[256,1024]{1,0:T(8,128)} %get-tuple-element.22), channel_id=1, source_target_pairs={{0,8},{1,9},{2,10},{3,11},{4,12},{5,13},{6,14},{7,15}} | collective-permute-start | bytes 3145736 | tf_op jit(solution)/shard_map/ppermute | solution.py:185
  245.2 69.5 %collective-permute-start.9 = (f32[256,1024]{1,0:T(8,128)}, f32[256,1024]{1,0:T(8,128)}, u32[]{:S(2)}, u32[]{:S(2)}) collective-permute-start(f32[256,1024]{1,0:T(8,128)} %get-tuple-element.22), channel_id=1, source_target_pairs={{24,16},{25,17},{26,18},{27,19},{28,20},{29,21},{30,22},{31,23}} | collective-permute-start | bytes 3145736 | tf_op jit(solution)/shard_map/ppermute | solution.py:186
  250.0 67.1 %collective-permute-start.13 = (f32[256,1024]{1,0:T(8,128)}, f32[256,1024]{1,0:T(8,128)}, u32[]{:S(2)}, u32[]{:S(2)}) collective-permute-start(f32[256,1024]{1,0:T(8,128)} %get-tuple-element.69), channel_id=1, source_target_pairs={{0,8},{8,16},{1,9},{9,17},{2,10},{10,18},{3,11},{11,19},{4,12},{12... | collective-permute-start | bytes 3145736 | tf_op jit(solution)/shard_map/ppermute | solution.py:185
  252.3 67.2 %collective-permute-start.16 = (f32[256,1024]{1,0:T(8,128)S(1)}, f32[256,1024]{1,0:T(8,128)}, u32[]{:S(2)}, u32[]{:S(2)}) collective-permute-start(f32[256,1024]{1,0:T(8,128)S(1)} %get-tuple-element.70), channel_id=1, source_target_pairs={{16,8},{24,16},{17,9},{25,17},{18,10},{26,18},{19,11},{27,19},{20,... | collective-permute-start | bytes 3145736 | tf_op jit(solution)/shard_map/ppermute | solution.py:186
  274.6 69.2 %collective-permute-start.19 = (f32[256,1024]{1,0:T(8,128)}, f32[256,1024]{1,0:T(8,128)}, u32[]{:S(2)}, u32[]{:S(2)}) collective-permute-start(f32[256,1024]{1,0:T(8,128)} %get-tuple-element.71), channel_id=1, source_target_pairs={{0,8},{8,16},{1,9},{9,17},{2,10},{10,18},{3,11},{11,19},{4,12},{12... | collective-permute-start | bytes 3145736 | tf_op jit(solution)/shard_map/ppermute | solution.py:185
  276.9 68.3 %collective-permute-start.22 = (f32[256,1024]{1,0:T(8,128)S(1)}, f32[256,1024]{1,0:T(8,128)}, u32[]{:S(2)}, u32[]{:S(2)}) collective-permute-start(f32[256,1024]{1,0:T(8,128)S(1)} %get-tuple-element.72), channel_id=1, source_target_pairs={{16,8},{24,16},{17,9},{25,17},{18,10},{26,18},{19,11},{27,19},{20,... | collective-permute-start | bytes 3145736 | tf_op jit(solution)/shard_map/ppermute | solution.py:186
  316.3 38.3 %collective-permute-start.10 = (f32[256,1024]{1,0:T(8,128)S(1)}, f32[256,1024]{1,0:T(8,128)S(1)}, u32[]{:S(2)}, u32[]{:S(2)}) collective-permute-start(f32[256,1024]{1,0:T(8,128)S(1)} %get-tuple-element.68), channel_id=1, source_target_pairs={{16,8},{24,16},{17,9},{25,17},{18,10},{26,18},{19,11},{27,19},{20,... | collective-permute-start | bytes 3145736 | tf_op jit(solution)/shard_map/ppermute | solution.py:186
  317.1 38.8 %collective-permute-start.7 = (f32[256,1024]{1,0:T(8,128)S(1)}, f32[256,1024]{1,0:T(8,128)}, u32[]{:S(2)}, u32[]{:S(2)}) collective-permute-start(f32[256,1024]{1,0:T(8,128)S(1)} %get-tuple-element.67), channel_id=1, source_target_pairs={{0,8},{8,16},{1,9},{9,17},{2,10},{10,18},{3,11},{11,19},{4,12},{12... | collective-permute-start | bytes 3145736 | tf_op jit(solution)/shard_map/ppermute | solution.py:185
  322.4 42.0 %collective-permute-start.14 = (f32[256,1024]{1,0:T(8,128)S(1)}, f32[256,1024]{1,0:T(8,128)}, u32[]{:S(2)}, u32[]{:S(2)}) collective-permute-start(f32[256,1024]{1,0:T(8,128)S(1)} %get-tuple-element.63), channel_id=1, source_target_pairs={{0,8},{8,16},{16,24},{1,9},{9,17},{17,25},{2,10},{10,18},{18,26},{... | collective-permute-start | bytes 3145736 | tf_op jit(solution)/shard_map/ppermute | solution.py:185
  343.8 79.3 %collective-permute-start.17 = (f32[256,1024]{1,0:T(8,128)}, f32[256,1024]{1,0:T(8,128)}, u32[]{:S(2)}, u32[]{:S(2)}) collective-permute-start(f32[256,1024]{1,0:T(8,128)} %get-tuple-element.64), channel_id=1, source_target_pairs={{8,0},{16,8},{24,16},{9,1},{17,9},{25,17},{10,2},{18,10},{26,18},{... | collective-permute-start | bytes 3145736 | tf_op jit(solution)/shard_map/ppermute | solution.py:186
  349.1 74.1 %collective-permute-start.20 = (f32[256,1024]{1,0:T(8,128)}, f32[256,1024]{1,0:T(8,128)}, u32[]{:S(2)}, u32[]{:S(2)}) collective-permute-start(f32[256,1024]{1,0:T(8,128)} %get-tuple-element.65), channel_id=1, source_target_pairs={{0,8},{8,16},{16,24},{1,9},{9,17},{17,25},{2,10},{10,18},{18,26},{... | collective-permute-start | bytes 3145736 | tf_op jit(solution)/shard_map/ppermute | solution.py:185
  354.6 68.5 %collective-permute-start.23 = (f32[256,1024]{1,0:T(8,128)}, f32[256,1024]{1,0:T(8,128)}, u32[]{:S(2)}, u32[]{:S(2)}) collective-permute-start(f32[256,1024]{1,0:T(8,128)} %get-tuple-element.66), channel_id=1, source_target_pairs={{8,0},{16,8},{24,16},{9,1},{17,9},{25,17},{10,2},{18,10},{26,18},{... | collective-permute-start | bytes 3145736 | tf_op jit(solution)/shard_map/ppermute | solution.py:186
  359.4 63.7 %collective-permute-start.11 = (f32[256,1024]{1,0:T(8,128)}, f32[256,1024]{1,0:T(8,128)}, u32[]{:S(2)}, u32[]{:S(2)}) collective-permute-start(f32[256,1024]{1,0:T(8,128)} %get-tuple-element.62), channel_id=1, source_target_pairs={{8,0},{16,8},{24,16},{9,1},{17,9},{25,17},{10,2},{18,10},{26,18},{... | collective-permute-start | bytes 3145736 | tf_op jit(solution)/shard_map/ppermute | solution.py:186
  364.4 58.7 %collective-permute-start.8 = (f32[256,1024]{1,0:T(8,128)}, f32[256,1024]{1,0:T(8,128)}, u32[]{:S(2)}, u32[]{:S(2)}) collective-permute-start(f32[256,1024]{1,0:T(8,128)} %get-tuple-element.61), channel_id=1, source_target_pairs={{0,8},{8,16},{16,24},{1,9},{9,17},{17,25},{2,10},{10,18},{18,26},{... | collective-permute-start | bytes 3145736 | tf_op jit(solution)/shard_map/ppermute | solution.py:185
  (16 other events, 229.9 us)
Sparse Core Ops, SparseCore 0:
  74.3 59.6 all-gather.14
  136.5 45.5 all-gather.12
  183.9 45.4 all-gather.10
  231.2 45.5 all-gather.8

commit v2 on v1

v2 whole, which is shorter than its diff:
```python
import functools

import jax
import jax.numpy as jnp
from jax import lax
from jax.experimental import pallas as pl
from jax.experimental.pallas import tpu as pltpu
from jax.sharding import PartitionSpec as P

time_step = 0.5
kerr_rate = 1.0
pump_rate = 0.6
detuning = 0.4
coupling_gain = 1.5

CHUNKS = 2
SHARES = 2
WORK = 1
VMEM = 56 * 2**20
f32, bf16 = jnp.float32, jnp.bfloat16


def halves(x):
    high = x.astype(bf16)
    return high, (x - high.astype(f32)).astype(bf16)


def products(split_ref, c_ref, add_ref, o_ref, share):
    k, (h, of), depth = pl.program_id(1), share, c_ref.shape[0]
    columns = pl.ds(pl.multiple_of((k * of + h) * depth, depth), depth)
    high, low = halves(c_ref[...])
    p_high = split_ref[0, :, columns]
    part = jnp.dot(p_high, high, preferred_element_type=f32)
    part += jnp.dot(split_ref[1, :, columns], high, preferred_element_type=f32)
    part += jnp.dot(p_high, low, preferred_element_type=f32)

    @pl.when(k == 0)
    def _():
        o_ref[...] = part if add_ref is None else add_ref[...] + part

    @pl.when(k > 0)
    def _():
        o_ref[...] += part


def put(split_ref, piece, row, column):
    rows, columns = pl.ds(row, piece.shape[0]), pl.ds(column, piece.shape[1])
    split_ref[0, rows, columns], split_ref[1, rows, columns] = halves(piece)


def opening_kernel(parts, share, more, *refs):
    offsets, pieces, (c_ref, *refs) = refs[0], refs[1 : -3 - 2 * more], refs[-3 - 2 * more :]
    o_ref, split_ref = refs[-2:]
    sites = len(pieces) // parts

    @pl.when((pl.program_id(0) == 0) & (pl.program_id(1) == 0))
    def _():
        if more:
            split_ref[...] = refs[1][...]
        for m in range(sites):
            for d in range(parts):
                piece = pieces[m * parts + d][...]
                row = pl.multiple_of(offsets[m], piece.shape[0])
                column = pl.multiple_of(offsets[sites + d], piece.shape[1])
                put(split_ref, piece, row, column)

    products(split_ref, c_ref, refs[0] if more else None, o_ref, share)


def split_kernel(added, split_ref, c_ref, *refs):
    products(split_ref, c_ref, refs[0] if added else None, refs[-1], (0, 1))


def whole_kernel(added, block_ref, c_ref, *refs):
    o_ref, split_ref = refs[-2:]
    k, depth = pl.program_id(1), c_ref.shape[0]

    @pl.when(pl.program_id(0) == 0)
    def _():
        for j in range(block_ref.shape[0]):
            put(split_ref, block_ref[j, k], j * block_ref.shape[2], pl.multiple_of(k * depth, depth))

    products(split_ref, c_ref, refs[0] if added else None, o_ref, (0, 1))


def step_kernel(terms, x_ref, y_ref, *refs):
    coupled = refs[0][...]
    for term in refs[1:terms]:
        coupled += term[...]
    x, y = x_ref[...], y_ref[...]
    radius = x * x + y * y
    y_next = y + time_step * (-(kerr_rate * radius - pump_rate + detuning) * x + coupling_gain * coupled)
    radius_next = x * x + y_next * y_next
    refs[-2][...] = x + time_step * (kerr_rate * radius_next + pump_rate + detuning) * y_next
    refs[-1][...] = y_next


def oscillate(terms, positions, momenta, lanes, outs):
    rows, width = positions.shape[0], lanes.stop - lanes.start
    tile = tile_of(width)
    there = pl.BlockSpec((rows, tile), lambda i: (0, lanes.start // tile + i))
    here = pl.BlockSpec((rows, tile), lambda i: (0, i))
    first = 2 + len(terms)
    return pl.pallas_call(
        functools.partial(step_kernel, len(terms)),
        grid=(width // tile,),
        in_specs=[there, there] + [here] * len(terms) + [pl.BlockSpec(memory_space=pl.ANY)] * len(outs),
        out_specs=[there, there],
        out_shape=[jax.ShapeDtypeStruct(positions.shape, f32)] * 2,
        input_output_aliases={first + i: i for i in range(len(outs))},
        name="oscillate",
    )(positions, momenta, *terms, *outs)


def tile_of(width):
    return max(t for t in range(128, 513, 128) if width % t == 0)


def call(kernel, operands, couplings, lanes, parts, rows, share=(0, 1), add=(), offsets=None, keep=False):
    h, of = share
    start, width = lanes.start, lanes.stop - lanes.start
    depth = couplings.shape[0] // (parts * of)
    tile = tile_of(width)

    def whole(x):
        return pl.BlockSpec(x.shape, lambda i, k, *_: (0,) * len(x.shape), pipeline_mode=pl.Buffered(1))

    result = pl.BlockSpec((rows, tile), lambda i, k, *_: (0, i))
    couple = pl.BlockSpec((depth, tile), lambda i, k, *_: (k * of + h, start // tile + i))
    in_specs, values = [whole(x) for x in operands] + [couple], [*operands, couplings]
    in_specs += [result if i == 0 else whole(x) for i, x in enumerate(add)]
    values += add
    out_shape, out_specs = [jax.ShapeDtypeStruct((rows, width), f32)], [result]
    split = jax.ShapeDtypeStruct((2, rows, couplings.shape[0]), bf16)
    if keep:
        out_shape.append(split)
        out_specs.append(pl.BlockSpec(split.shape, lambda i, k, *_: (0, 0, 0)))
    out = pl.pallas_call(
        kernel,
        grid_spec=pltpu.PrefetchScalarGridSpec(
            num_scalar_prefetch=int(offsets is not None),
            grid=(width // tile, parts),
            in_specs=in_specs,
            out_specs=out_specs,
        ),
        out_shape=out_shape,
        compiler_params=pltpu.CompilerParams(vmem_limit_bytes=VMEM),
        cost_estimate=pl.CostEstimate(flops=WORK * rows * width * depth * parts, bytes_accessed=0, transcendentals=0),
        name="products",
    )(*(() if offsets is None else (offsets,)), *values)
    return out if keep else out[0]


def after(x, *others):
    return lax.optimization_barrier((x, *others))[0]


class Plan:
    def __init__(self, n, cols):
        self.n, self.cols, self.ratio = n, cols, cols // n
        assert self.ratio * n == cols
        self.order = [[self.shift(z, a) for a in range(n - 1, -1, -1)] for z in range(n)]
        self.slot = [[self.order[z].index(s) for s in range(n)] for z in range(n)]

    def shift(self, a, b):
        return a ^ b if self.n & (self.n - 1) == 0 else (a + b) % self.n

    def unshift(self, a, b):
        return a ^ b if self.n & (self.n - 1) == 0 else (a - b) % self.n

    def messages(self, t, k):
        n, rounds = self.n, []
        for z in range(t + 1):
            if z < n - 1 and self.slot[z][n - 1 - t + z] == k:
                pair = [(z, z + 1), (n - 1 - z, n - 2 - z)]
                for others in rounds:
                    both = others + pair
                    if len({a for a, _ in both}) == len({b for _, b in both}) == len(both):
                        others += pair
                        break
                else:
                    rounds.append(pair)
        return rounds

    def sources(self, t, k):
        n, out = self.n, {}
        for pairs in self.messages(t, k):
            out.update((a, 2 * a - b if 0 <= 2 * a - b < n else None) for a, b in pairs)
        if k == t:
            for later in range(t + 1, n - 1):
                for pairs in self.messages(later, k):
                    out.update((a, None) for a, _ in pairs)
        return out

    def site_pairs(self, m):
        r = self.ratio
        return [(q * r + c, self.shift(q, m) * r + c) for q in range(self.n) for c in range(r)]


def shift(plan, a, b):
    return a ^ b if plan.n & (plan.n - 1) == 0 else lax.rem(a + b, plan.n)


def unshift(plan, a, b):
    return a ^ b if plan.n & (plan.n - 1) == 0 else lax.rem(a - b + plan.n, plan.n)


def one_of(values, index):
    out = values[0]
    for i in range(1, len(values)):
        out = jnp.where(index == i, values[i], out)
    return out


def pick(values, choice, index):
    used = sorted({c for c in choice if c is not None})
    out = values[used[0]]
    for c in used[1:]:
        mine = functools.reduce(jnp.logical_or, [index == i for i, v in enumerate(choice) if v == c])
        out = jnp.where(mine, values[c], out)
    return out


def spread_sites(plan, positions, col, start, depth):
    n = plan.n
    site = col // plan.ratio
    rows = positions.shape[0] // n
    arrived = []
    for m in range(n):
        part = lax.dynamic_slice(positions, (shift(plan, site, m) * rows, start), (rows, depth))
        arrived.append(part if m == 0 else lax.ppermute(part, "col", plan.site_pairs(m)))
    return arrived


def exchange_rows(plan, k, arrived, row, col, *before):
    n = plan.n
    target = [[plan.order[z][k] for z in range(n)].index(r) for r in range(n)]
    part = one_of(arrived, unshift(plan, col // plan.ratio, one_of(target, row)))
    if before:
        part = after(part, *before)
    pairs = [(r, target[r]) for r in range(n)]
    return lax.ppermute(part, "row", pairs) if any(a != b for a, b in pairs) else part


def gather_plane(plan, part):
    whole = lax.all_gather(part, "col", axis=0, tiled=False)
    return whole.reshape(plan.n, plan.ratio, *part.shape)


def gather_sites(plan, part):
    return [part if m == 0 else lax.ppermute(part, "col", plan.site_pairs(m)) for m in range(plan.n)]


def gather_parts(plan, pieces):
    r = plan.ratio
    turns = [[(q * r + c, q * r + (c + d) % r) for q in range(plan.n) for c in range(r)] for d in range(r)]
    return [p if d == 0 else lax.ppermute(p, "col", turns[d]) for p in pieces for d in range(r)]


def piece_offsets(plan, rows, depth, start, col):
    n, r = plan.n, plan.ratio
    site, part = col // r, lax.rem(col, r)
    starts = [unshift(plan, site, m) * rows for m in range(n)]
    starts += [lax.rem(part - d + r, r) * depth + start for d in range(r)]
    return jnp.stack(starts).astype(jnp.int32)


class Sums:
    def __init__(self):
        self.arrays = []

    def add(self, array, pairs):
        self.arrays.append((array, {b: a for a, b in pairs}))

    def carried(self, wanted, row):
        def serves(heard, z):
            return heard.get(z) == wanted[z]

        for array, heard in self.arrays:
            if all(serves(heard, z) for z in wanted):
                return array
        out = None
        for array, heard in self.arrays:
            mine = functools.reduce(
                jnp.logical_or, [row == z for z in wanted if wanted[z] is not None and serves(heard, z)], False
            )
            kept = jnp.where(mine, array, 0.0)
            out = kept if out is None else out + kept
        return out


def per_device(plan, positions, momenta, couplings):
    n = plan.n
    row, col = lax.axis_index("row"), lax.axis_index("col")
    width = positions.shape[1]
    chunk = width // CHUNKS
    lanes = [slice(c * chunk, (c + 1) * chunk) for c in range(CHUNKS)]

    depth = width // SHARES
    spread = [spread_sites(plan, positions, col, h * depth, depth) for h in range(SHARES)]
    own = []
    for h in range(SHARES):
        own.append(exchange_rows(plan, 0, spread[h], row, col, *own[-1:]))
    opening = [gather_sites(plan, part) for part in own]
    spread = [jnp.concatenate(share, axis=1) for share in zip(*spread)]
    for k in range(1, n):
        own.append(exchange_rows(plan, k, spread, row, col, *own[SHARES - 1 :][: 1 if k < n - 1 else None]))
    own = own[SHARES - 1 :]

    partial = [[None] * CHUNKS for _ in range(n)]
    sums = [[Sums() for _ in range(CHUNKS)] for _ in range(n)]
    rows, so_far, outs = positions.shape[0], None, []
    for h in range(SHARES):
        pieces = opening[h]
        if h:
            couplings = after(couplings, so_far[0], own[SHARES])
            pieces = [after(piece, so_far[0]) for piece in pieces]
        pieces = gather_parts(plan, pieces)
        so_far = call(
            functools.partial(opening_kernel, plan.ratio, (h, SHARES), so_far is not None),
            pieces,
            couplings,
            lanes[0],
            plan.ratio,
            rows,
            share=(h, SHARES),
            add=so_far or (),
            offsets=piece_offsets(plan, rows // n, width, h * depth, col),
            keep=True,
        )
    partial[0][0], block = so_far
    own = [after(part, partial[0][0], own[-2]) for part in own]
    gathered = [None] + [gather_plane(plan, part) for part in own[1:]]
    couplings = after(couplings, *own[1:])
    last = partial[0][0]
    for t in range(n):
        for c, span in enumerate(lanes):
            add = []
            if 0 < t < n - 1:
                add = [sums[t - 1][c].carried(plan.sources(t, t), row)]
            if t or c:
                before = [array for array, _ in sums[t - 1][c].arrays] if 0 < t < n - 1 else []
                couplings = after(couplings, last, *before)
                first = c == 0 and t > 0
                operand = gathered[t] if first else block
                kernel = functools.partial(whole_kernel if first else split_kernel, len(add))
                out = call(kernel, [operand], couplings, span, plan.ratio, rows, add=add, keep=first)
                last, block = out if first else (out, block)
                partial[t][c] = last
            for k in range(t + 1):
                mine = partial[t][c]
                if k < t:
                    if not plan.messages(t, k):
                        continue
                    mine = after(partial[k][c], partial[t][c]) + sums[t - 1][c].carried(plan.sources(t, k), row)
                for pairs in plan.messages(t, k):
                    sums[t][c].add(lax.ppermute(mine, "row", pairs), pairs)
            if t == n - 1:
                terms = [last] + [array for array, _ in sums[n - 2][c].arrays]
                outs = oscillate(terms, positions, momenta, span, outs)
                couplings = after(couplings, outs[0])
    return outs


def solution(mesh):
    placed = (P("row", "col"), P("row", "col"), P("row", "col"))
    plan = Plan(mesh.shape["row"], mesh.shape["col"])

    def step(positions, momenta, couplings):
        return per_device(plan, positions, momenta, couplings)

    return jax.shard_map(
        step,
        mesh=mesh,
        in_specs=placed,
        out_specs=(P("row", "col"), P("row", "col")),
        check_vma=False,
    )
```

time: 446 us -> 371 us (0.83); the launches traced: 438 us -> 370 us
  waiting for transfers between devices: 108 us -> 72.9 us
  other arithmetic: 28.9 us -> 9.92 us
  starting transfers between devices: 68.7 us -> 53.3 us
    ppermute x21 -> x28, waiting for transfers between devices: 73.3 us -> 37.7 us  [the longest x4 16.1 us: exchange_rows(): lax.ppermute(part, 'row', pairs)]
    ppermute x21 -> x28, starting transfers between devices: 64.1 us -> 45.1 us  [the longest x10 27.3 us: per_device(): sums[t][c].add(lax.ppermute(mine, 'row', pairs), pairs)]
    add x7 -> x2, other arithmetic: 22.8 us -> 4.17 us  [per_device(): after(partial[k][c], partial[t][c])]
    ppermute x3 -> x6, waiting for transfers between devices: 34.4 us -> 27.3 us  [spread_sites(): lax.ppermute(part, 'col', plan.site_pairs(m))]
    all_gather x4 -> x3, waiting for transfers between devices: 0.08 us -> 6.49 us  [gather_plane(): whole = lax.all_gather(part, 'col', axis=0, tiled=False)]
    pallas_call x12 -> x11, Pallas kernels: 212 us -> 214 us  [the longest x9 202 us: call(): pl.pallas_call(kernel, grid_spec=pltpu.PrefetchScalarGridSpec(num_scalar_...]
  transfers between devices with their start and end apart: 28 -> 37, of which waited for: 7 -> 13; matrix products, arithmetic and copies ran while one was open for 4% -> 2% of each run, Pallas kernels for 48% -> 56%
where the time goes in v2:
time: 371 us; the launch traced here: 370 us
  Pallas kernels  214 us (58%)
  waiting for transfers between devices  72.9 us (20%)
  starting transfers between devices  53.3 us (14%)
  between operations  14 us (4%)
  other arithmetic  9.92 us (3%)
  local copies, waits for them, and re-layouts  5.59 us (2%)
    pallas_call x9, Pallas kernels, call(): pl.pallas_call(kernel, grid_spec=pltpu.PrefetchScalarGridSpec(num_scalar_...  202 us
    ppermute x6, waiting for transfers between devices, spread_sites(): lax.ppermute(part, 'col', plan.site_pairs(m))  27.3 us
    ppermute x10, starting transfers between devices, per_device(): sums[t][c].add(lax.ppermute(mine, 'row', pairs), pairs)  27.3 us
    ppermute x4, waiting for transfers between devices, exchange_rows(): lax.ppermute(part, 'row', pairs)  16.1 us
    ppermute x10, waiting for transfers between devices, per_device(): sums[t][c].add(lax.ppermute(mine, 'row', pairs), pairs)  15.1 us
    pallas_call x2, Pallas kernels, oscillate(): pl.pallas_call(functools.partial(step_kernel, len(terms)), grid=(width //...  12 us
    ppermute x4, starting transfers between devices, exchange_rows(): lax.ppermute(part, 'row', pairs)  10.1 us
    ppermute x6, starting transfers between devices, spread_sites(): lax.ppermute(part, 'col', plan.site_pairs(m))  8.09 us
  transfers between devices with their start and end apart: 37, of which 13 were waited for; matrix products, arithmetic and copies ran while one was open for 2% of the time, Pallas kernels for 56%

profile of v2, /device:TPU:0, one launch (start us, length us, event | category | flops | bytes accessed | tf_op | source)
XLA Modules:
  0.0 369.9 jit_solution(5205623702249031427)
XLA Ops:
  13.2 9.3 %collective-permute-done = f32[64,1536]{1,0:T(8,128)S(1)} collective-permute-done((f32[64,1536]{1,0:T(8,128)S(1)}, f32[64,1536]{1,0:T(8,128)S(1)}, u32[]{:S(2)}, u32[]{:S(2)}) %collective-permute-start) | collective-permute-done | bytes 393248 | tf_op jit(solution)/shard_map/ppermute | solution.py:231
  22.5 7.6 %collective-permute-done.2 = f32[64,1536]{1,0:T(8,128)S(1)} collective-permute-done((f32[64,1536]{1,0:T(8,128)S(1)}, f32[64,1536]{1,0:T(8,128)S(1)}, u32[]{:S(2)}, u32[]{:S(2)}) %collective-permute-start.2) | collective-permute-done | bytes 393248 | tf_op jit(solution)/shard_map/ppermute | solution.py:231
  40.9 6.3 %collective-permute-done.6.refs_1_ = f32[64,1536]{1,0:T(8,128)} collective-permute-done((f32[64,1536]{1,0:T(8,128)}, f32[64,1536]{1,0:T(8,128)}, u32[]{:S(2)}, u32[]{:S(2)}) %collective-permute-start.6) | collective-permute-done | bytes 393248 | tf_op jit(solution)/shard_map/ppermute | solution.py:242
  50.6 7.4 %collective-permute-done.3 = f32[64,1536]{1,0:T(8,128)} collective-permute-done((f32[64,1536]{1,0:T(8,128)}, f32[64,1536]{1,0:T(8,128)}, u32[]{:S(2)}, u32[]{:S(2)}) %collective-permute-start.3) | collective-permute-done | bytes 393248 | tf_op jit(solution)/shard_map/ppermute | solution.py:231
  62.3 5.2 %collective-permute-done.11.refs_3_ = f32[64,1536]{1,0:T(8,128)S(1)} collective-permute-done((f32[64,1536]{1,0:T(8,128)}, f32[64,1536]{1,0:T(8,128)S(1)}, u32[]{:S(2)}, u32[]{:S(2)}) %collective-permute-start.11) | collective-permute-done | bytes 393248 | tf_op jit(solution)/shard_map/ppermute | solution.py:251
  72.5 6.1 %collective-permute-start.9 = (f32[64,3072]{1,0:T(8,128)}, f32[64,3072]{1,0:T(8,128)S(1)}, u32[]{:S(2)}, u32[]{:S(2)}) collective-permute-start(f32[64,3072]{1,0:T(8,128)} %get-tuple-element.39), channel_id=1, source_target_pairs={{0,8},{8,0},{16,24},{24,16},{1,9},{9,1},{17,25},{25,17},{2,10},{10... | collective-permute-start | bytes 2359304 | tf_op jit(solution)/shard_map/ppermute | solution.py:242
  83.1 17.0 %products.9 = (f32[256,1536]{1,0:T(8,128)}, bf16[2,256,6144]{2,1,0:T(8,128)(2,1)}) custom-call(s32[6]{0:T(128)} %stack.43.refs_0_, f32[64,1536]{1,0:T(8,128)} %collective-permute-done.6.refs_1_, f32[64,1536]{1,0:T(8,128)} %copy-done.11, f32[64,1536]{1,0:T(8,128)} %copy-done.6, f32[64,1536]{1,0:T(8,128)} %copy-done.13, f32[64,1536]{1,0:T(8,128)} %copy-done.7, ...), custom_call_target="tpu_custom_call" | custom-call | flops 1207959552 | tf_op jit(solution)/shard_map/products/pallas_call | solution.py:138
  100.8 6.9 %collective-permute-done.9 = f32[64,3072]{1,0:T(8,128)S(1)} collective-permute-done((f32[64,3072]{1,0:T(8,128)}, f32[64,3072]{1,0:T(8,128)S(1)}, u32[]{:S(2)}, u32[]{:S(2)}) %collective-permute-start.9) | collective-permute-done | bytes 786464 | tf_op jit(solution)/shard_map/ppermute | solution.py:242
  109.8 19.7 %products.10 = (f32[256,1536]{1,0:T(8,128)}, bf16[2,256,6144]{2,1,0:T(8,128)(2,1)}) custom-call(s32[6]{0:T(128)} %stack.40.refs_0_, f32[64,1536]{1,0:T(8,128)} %collective-permute-done.7.refs_1_, f32[64,1536]{1,0:T(8,128)} %collective-permute-done.17.refs_2_, f32[64,1536]{1,0:T(8,128)} %copy-done.12, f32[64,1536]{1,0:T(8,128)} %collective-permute-done.19.refs_4_, ...), custom_call_target="tpu_custom_call" | custom-call | flops 1207959552 | tf_op jit(solution)/shard_map/products/pallas_call | solution.py:138
  132.6 22.9 %products.11 = f32[256,1536]{1,0:T(8,128)} custom-call(bf16[2,256,6144]{2,1,0:T(8,128)(2,1)} %get-tuple-element.54.split_ref, f32[6144,3072]{1,0:T(8,128)} %c_ref.6), custom_call_target="tpu_custom_call" | custom-call | flops 2415919104 | tf_op jit(solution)/shard_map/products/pallas_call | solution.py:138
  158.0 9.3 %collective-permute-done.24.refs_0_ = f32[256,1536]{1,0:T(8,128)S(1)} collective-permute-done((f32[256,1536]{1,0:T(8,128)S(1)}, f32[256,1536]{1,0:T(8,128)S(1)}, u32[]{:S(2)}, u32[]{:S(2)}) %collective-permute-start.24) | collective-permute-done | bytes 1572896 | tf_op jit(solution)/shard_map/ppermute | solution.py:357
  167.3 6.5 %all-gather.9.cloned.1.call-done = f32[512,3072]{1,0:T(8,128)} async-done(((f32[64,3072]{1,0:T(8,128)}), f32[512,3072]{1,0:T(8,128)}) %all-gather.9.cloned.1.call-update) | async-done | bytes 6291472 | tf_op jit(solution)/shard_map/all_gather | solution.py:246
  173.8 25.2 %products.12 = (f32[256,1536]{1,0:T(8,128)}, bf16[2,256,6144]{2,1,0:T(8,128)(2,1)}) custom-call(f32[4,2,64,3072]{3,2,1,0:T(8,128)} %bitcast.13, f32[6144,3072]{1,0:T(8,128)} %c_ref.6, f32[256,1536]{1,0:T(8,128)} %copy-done.4), custom_call_target="tpu_custom_call" | custom-call | flops 2415919104 | tf_op jit(solution)/shard_map/products/pallas_call | solution.py:138
  199.0 4.5 %collective-permute-start.26 = (f32[256,1536]{1,0:T(8,128)}, f32[256,1536]{1,0:T(8,128)}, u32[]{:S(2)}, u32[]{:S(2)}) collective-permute-start(f32[256,1536]{1,0:T(8,128)} %get-tuple-element.56), channel_id=1, source_target_pairs={{0,8},{24,16},{1,9},{25,17},{2,10},{26,18},{3,11},{27,19},{4,12},{... | collective-permute-start | bytes 4718600 | tf_op jit(solution)/shard_map/ppermute | solution.py:357
  205.4 22.5 %products.13 = f32[256,1536]{1,0:T(8,128)} custom-call(bf16[2,256,6144]{2,1,0:T(8,128)(2,1)} %get-tuple-element.58.split_ref, f32[6144,3072]{1,0:T(8,128)} %c_ref.6, f32[256,1536]{1,0:T(8,128)} %collective-permute-done.25.refs_0_), custom_call_target="tpu_custom_call" | custom-call | flops 2415919104 | tf_op jit(solution)/shard_map/products/pallas_call | solution.py:138
  231.6 5.8 %collective-permute-done.26 = f32[256,1536]{1,0:T(8,128)} collective-permute-done((f32[256,1536]{1,0:T(8,128)}, f32[256,1536]{1,0:T(8,128)}, u32[]{:S(2)}, u32[]{:S(2)}) %collective-permute-start.26) | collective-permute-done | bytes 1572896 | tf_op jit(solution)/shard_map/ppermute | solution.py:357
  237.4 25.2 %products.14 = (f32[256,1536]{1,0:T(8,128)}, bf16[2,256,6144]{2,1,0:T(8,128)(2,1)}) custom-call(f32[4,2,64,3072]{3,2,1,0:T(8,128)} %bitcast.12, f32[6144,3072]{1,0:T(8,128)} %c_ref.6, f32[256,1536]{1,0:T(8,128)} %collective-permute-done.27.refs_0_), custom_call_target="tpu_custom_call" | custom-call | flops 2415919104 | tf_op jit(solution)/shard_map/products/pallas_call | solution.py:138
  267.3 5.8 %collective-permute-start.31 = (f32[256,1536]{1,0:T(8,128)}, f32[256,1536]{1,0:T(8,128)}, u32[]{:S(2)}, u32[]{:S(2)}) collective-permute-start(f32[256,1536]{1,0:T(8,128)} %get-tuple-element.60), channel_id=1, source_target_pairs={{0,8},{24,16},{16,24},{8,0},{1,9},{25,17},{17,25},{9,1},{2,10},{26... | collective-permute-start | bytes 4718600 | tf_op jit(solution)/shard_map/ppermute | solution.py:357
  273.0 22.5 %products.15 = f32[256,1536]{1,0:T(8,128)} custom-call(bf16[2,256,6144]{2,1,0:T(8,128)(2,1)} %get-tuple-element.62.split_ref, f32[6144,3072]{1,0:T(8,128)} %c_ref.6, f32[256,1536]{1,0:T(8,128)} %collective-permute-done.29.refs_0_), custom_call_target="tpu_custom_call" | custom-call | flops 2415919104 | tf_op jit(solution)/shard_map/products/pallas_call | solution.py:138
  297.9 4.5 %collective-permute-start.33 = (f32[256,1536]{1,0:T(8,128)}, f32[256,1536]{1,0:T(8,128)S(1)}, u32[]{:S(2)}, u32[]{:S(2)}) collective-permute-start(f32[256,1536]{1,0:T(8,128)} %products.15), channel_id=1, source_target_pairs={{0,8},{24,16},{16,24},{8,0},{1,9},{25,17},{17,25},{9,1},{2,10},{26... | collective-permute-start | bytes 4718600 | tf_op jit(solution)/shard_map/ppermute | solution.py:357
  302.4 25.0 %products.16 = (f32[256,1536]{1,0:T(8,128)}, bf16[2,256,6144]{2,1,0:T(8,128)(2,1)}) custom-call(f32[4,2,64,3072]{3,2,1,0:T(8,128)} %bitcast.11, f32[6144,3072]{1,0:T(8,128)} %c_ref.6), custom_call_target="tpu_custom_call" | custom-call | flops 2415919104 | tf_op jit(solution)/shard_map/products/pallas_call | solution.py:138
  327.4 6.1 %oscillate.2 = (f32[256,3072]{1,0:T(8,128)}, f32[256,3072]{1,0:T(8,128)}) custom-call(f32[256,3072]{1,0:T(8,128)} %x_ref.3, f32[256,3072]{1,0:T(8,128)} %y_ref.3, f32[256,1536]{1,0:T(8,128)} %get-tuple-element.65.refs_0_, f32[256,1536]{1,0:T(8,128)} %collective-permute-done.30.refs_1_, f32[256,1536]{1,0:T(8,128)} %collective-permute-done.31.refs_2_), custom_call_target="tpu_custom_call" | custom-call | tf_op jit(solution)/shard_map/oscillate/pallas_call | solution.py:104
  333.5 22.2 %products.17.refs_0_ = f32[256,1536]{1,0:T(8,128)} custom-call(bf16[2,256,6144]{2,1,0:T(8,128)(2,1)} %get-tuple-element.64.split_ref, f32[6144,3072]{1,0:T(8,128)} %c_ref.6), custom_call_target="tpu_custom_call" | custom-call | flops 2415919104 | tf_op jit(solution)/shard_map/products/pallas_call | solution.py:138
  357.4 6.0 %oscillate.3 = (f32[256,3072]{1,0:T(8,128)}, f32[256,3072]{1,0:T(8,128)}) custom-call(f32[256,3072]{1,0:T(8,128)} %x_ref.3, f32[256,3072]{1,0:T(8,128)} %y_ref.3, f32[256,1536]{1,0:T(8,128)} %products.17.refs_0_, f32[256,1536]{1,0:T(8,128)} %copy-done.1, f32[256,1536]{1,0:T(8,128)} %copy-done.2, ...), custom_call_target="tpu_custom_call", output_to_operand_aliasing={{0}: (5, {}), {1}: (6, {})} | custom-call | tf_op jit(solution)/shard_map/oscillate/pallas_call | solution.py:104
  (110 shorter events, 56.5 us)
Async XLA Ops:
  7.2 166.6 %all-gather.9.cloned.1.call-start = ((), (), s32[]{:S(2)}) async-start(), calls=%async_computation.1 | async-start | bytes 7077888 | tf_op jit(solution)/shard_map/all_gather | solution.py:246
  13.0 17.8 %collective-permute-start.4 = (f32[64,1536]{1,0:T(8,128)S(1)}, f32[64,1536]{1,0:T(8,128)}, u32[]{:S(2)}, u32[]{:S(2)}) collective-permute-start(f32[64,1536]{1,0:T(8,128)S(1)} %get-tuple-element.82), channel_id=1, source_target_pairs={{0,2},{1,3},{2,0},{3,1},{4,6},{5,7},{6,4},{7,5},{8,10},{9,11},{10,... | collective-permute-start | bytes 1179656 | tf_op jit(solution)/shard_map/ppermute | solution.py:231
  39.2 18.9 %collective-permute-start.3 = (f32[64,1536]{1,0:T(8,128)}, f32[64,1536]{1,0:T(8,128)}, u32[]{:S(2)}, u32[]{:S(2)}) collective-permute-start(f32[64,1536]{1,0:T(8,128)} %get-tuple-element.80), channel_id=1, source_target_pairs={{0,4},{1,5},{2,6},{3,7},{4,0},{5,1},{6,2},{7,3},{8,12},{9,13},{10,... | collective-permute-start | bytes 1179656 | tf_op jit(solution)/shard_map/ppermute | solution.py:231
  40.4 18.8 %collective-permute-start.5 = (f32[64,1536]{1,0:T(8,128)S(1)}, f32[64,1536]{1,0:T(8,128)}, u32[]{:S(2)}, u32[]{:S(2)}) collective-permute-start(f32[64,1536]{1,0:T(8,128)S(1)} %get-tuple-element.79), channel_id=1, source_target_pairs={{0,2},{1,3},{2,0},{3,1},{4,6},{5,7},{6,4},{7,5},{8,10},{9,11},{10,... | collective-permute-start | bytes 1179656 | tf_op jit(solution)/shard_map/ppermute | solution.py:231
  47.3 20.3 %collective-permute-start.11 = (f32[64,1536]{1,0:T(8,128)}, f32[64,1536]{1,0:T(8,128)S(1)}, u32[]{:S(2)}, u32[]{:S(2)}) collective-permute-start(f32[64,1536]{1,0:T(8,128)} %collective-permute-done.6.refs_1_), channel_id=1, source_target_pairs={{0,2},{1,3},{2,0},{3,1},{4,6},{5,7},{6,4},{7,5},{8,10},{9,11},{10,... | collective-permute-start | bytes 1179656 | tf_op jit(solution)/shard_map/ppermute | solution.py:251
  48.8 18.8 %collective-permute-start.13 = (f32[64,1536]{1,0:T(8,128)}, f32[64,1536]{1,0:T(8,128)S(1)}, u32[]{:S(2)}, u32[]{:S(2)}) collective-permute-start(f32[64,1536]{1,0:T(8,128)} %collective-permute-done.6.refs_1_), channel_id=1, source_target_pairs={{0,4},{1,5},{2,6},{3,7},{4,0},{5,1},{6,2},{7,3},{8,12},{9,13},{10,... | collective-permute-start | bytes 1179656 | tf_op jit(solution)/shard_map/ppermute | solution.py:251
  60.9 17.7 %collective-permute-start.15 = (f32[64,1536]{1,0:T(8,128)}, f32[64,1536]{1,0:T(8,128)S(1)}, u32[]{:S(2)}, u32[]{:S(2)}) collective-permute-start(f32[64,1536]{1,0:T(8,128)} %collective-permute-done.6.refs_1_), channel_id=1, source_target_pairs={{0,6},{1,7},{2,4},{3,5},{4,2},{5,3},{6,0},{7,1},{8,14},{9,15},{10,... | collective-permute-start | bytes 1179656 | tf_op jit(solution)/shard_map/ppermute | solution.py:251
  72.5 35.2 %collective-permute-start.9 = (f32[64,3072]{1,0:T(8,128)}, f32[64,3072]{1,0:T(8,128)S(1)}, u32[]{:S(2)}, u32[]{:S(2)}) collective-permute-start(f32[64,3072]{1,0:T(8,128)} %get-tuple-element.39), channel_id=1, source_target_pairs={{0,8},{8,0},{16,24},{24,16},{1,9},{9,1},{17,25},{25,17},{2,10},{10... | collective-permute-start | bytes 2359304 | tf_op jit(solution)/shard_map/ppermute | solution.py:242
  78.6 21.5 %collective-permute-start.22 = (f32[64,1536]{1,0:T(8,128)}, f32[64,1536]{1,0:T(8,128)S(1)}, u32[]{:S(2)}, u32[]{:S(2)}) collective-permute-start(f32[64,1536]{1,0:T(8,128)} %collective-permute-done.7.refs_1_), channel_id=1, source_target_pairs={{0,6},{1,7},{2,4},{3,5},{4,2},{5,3},{6,0},{7,1},{8,14},{9,15},{10,... | collective-permute-start | bytes 1179656 | tf_op jit(solution)/shard_map/ppermute | solution.py:251
  79.6 20.6 %collective-permute-start.20 = (f32[64,1536]{1,0:T(8,128)}, f32[64,1536]{1,0:T(8,128)S(1)}, u32[]{:S(2)}, u32[]{:S(2)}) collective-permute-start(f32[64,1536]{1,0:T(8,128)} %collective-permute-done.7.refs_1_), channel_id=1, source_target_pairs={{0,4},{1,5},{2,6},{3,7},{4,0},{5,1},{6,2},{7,3},{8,12},{9,13},{10,... | collective-permute-start | bytes 1179656 | tf_op jit(solution)/shard_map/ppermute | solution.py:251
  81.6 19.1 %collective-permute-start.18 = (f32[64,1536]{1,0:T(8,128)}, f32[64,1536]{1,0:T(8,128)S(1)}, u32[]{:S(2)}, u32[]{:S(2)}) collective-permute-start(f32[64,1536]{1,0:T(8,128)} %collective-permute-done.7.refs_1_), channel_id=1, source_target_pairs={{0,2},{1,3},{2,0},{3,1},{4,6},{5,7},{6,4},{7,5},{8,10},{9,11},{10,... | collective-permute-start | bytes 1179656 | tf_op jit(solution)/shard_map/ppermute | solution.py:251
  82.3 47.1 %collective-permute-start.8 = (f32[64,3072]{1,0:T(8,128)S(1)}, f32[64,3072]{1,0:T(8,128)}, u32[]{:S(2)}, u32[]{:S(2)}) collective-permute-start(f32[64,3072]{1,0:T(8,128)S(1)} %get-tuple-element.38), channel_id=1, source_target_pairs={{0,16},{8,24},{16,0},{24,8},{1,17},{9,25},{17,1},{25,9},{2,18},{10... | collective-permute-start | bytes 2359304 | tf_op jit(solution)/shard_map/ppermute | solution.py:242
  129.5 107.9 %all-gather.11.cloned.1.call-start = ((), (), s32[]{:S(2)}) async-start(), calls=%async_computation.2 | async-start | bytes 7077888 | tf_op jit(solution)/shard_map/all_gather | solution.py:246
  130.2 172.2 %all-gather.7.cloned.1.call-start = ((), (), s32[]{:S(2)}) async-start(), calls=%async_computation | async-start | bytes 7077888 | tf_op jit(solution)/shard_map/all_gather | solution.py:246
  131.0 36.3 %collective-permute-start.24 = (f32[256,1536]{1,0:T(8,128)S(1)}, f32[256,1536]{1,0:T(8,128)S(1)}, u32[]{:S(2)}, u32[]{:S(2)}) collective-permute-start(f32[256,1536]{1,0:T(8,128)S(1)} %copy-done.3), channel_id=1, source_target_pairs={{0,8},{24,16},{1,9},{25,17},{2,10},{26,18},{3,11},{27,19},{4,12},{... | collective-permute-start | bytes 4718600 | tf_op jit(solution)/shard_map/ppermute | solution.py:357
  155.6 49.8 %collective-permute-start.25 = (f32[256,1536]{1,0:T(8,128)}, f32[256,1536]{1,0:T(8,128)}, u32[]{:S(2)}, u32[]{:S(2)}) collective-permute-start(f32[256,1536]{1,0:T(8,128)} %products.11), channel_id=1, source_target_pairs={{0,8},{24,16},{1,9},{25,17},{2,10},{26,18},{3,11},{27,19},{4,12},{... | collective-permute-start | bytes 4718600 | tf_op jit(solution)/shard_map/ppermute | solution.py:357
  199.0 38.4 %collective-permute-start.26 = (f32[256,1536]{1,0:T(8,128)}, f32[256,1536]{1,0:T(8,128)}, u32[]{:S(2)}, u32[]{:S(2)}) collective-permute-start(f32[256,1536]{1,0:T(8,128)} %get-tuple-element.56), channel_id=1, source_target_pairs={{0,8},{24,16},{1,9},{25,17},{2,10},{26,18},{3,11},{27,19},{4,12},{... | collective-permute-start | bytes 4718600 | tf_op jit(solution)/shard_map/ppermute | solution.py:357
  203.5 33.9 %collective-permute-start.27 = (f32[256,1536]{1,0:T(8,128)}, f32[256,1536]{1,0:T(8,128)}, u32[]{:S(2)}, u32[]{:S(2)}) collective-permute-start(f32[256,1536]{1,0:T(8,128)} %get-tuple-element.56), channel_id=1, source_target_pairs={{8,16},{16,8},{9,17},{17,9},{10,18},{18,10},{11,19},{19,11},{12,20... | collective-permute-start | bytes 4718600 | tf_op jit(solution)/shard_map/ppermute | solution.py:357
  227.9 45.1 %collective-permute-start.28 = (f32[256,1536]{1,0:T(8,128)}, f32[256,1536]{1,0:T(8,128)S(1)}, u32[]{:S(2)}, u32[]{:S(2)}) collective-permute-start(f32[256,1536]{1,0:T(8,128)} %products.13), channel_id=1, source_target_pairs={{0,8},{24,16},{1,9},{25,17},{2,10},{26,18},{3,11},{27,19},{4,12},{... | collective-permute-start | bytes 4718600 | tf_op jit(solution)/shard_map/ppermute | solution.py:357
  229.8 43.3 %collective-permute-start.29 = (f32[256,1536]{1,0:T(8,128)}, f32[256,1536]{1,0:T(8,128)}, u32[]{:S(2)}, u32[]{:S(2)}) collective-permute-start(f32[256,1536]{1,0:T(8,128)} %products.13), channel_id=1, source_target_pairs={{8,16},{16,8},{9,17},{17,9},{10,18},{18,10},{11,19},{19,11},{12,20... | collective-permute-start | bytes 4718600 | tf_op jit(solution)/shard_map/ppermute | solution.py:357
  265.4 61.9 %collective-permute-start.30 = (f32[256,1536]{1,0:T(8,128)}, f32[256,1536]{1,0:T(8,128)}, u32[]{:S(2)}, u32[]{:S(2)}) collective-permute-start(f32[256,1536]{1,0:T(8,128)} %add.48), channel_id=1, source_target_pairs={{8,16},{16,8},{9,17},{17,9},{10,18},{18,10},{11,19},{19,11},{12,20... | collective-permute-start | bytes 4718600 | tf_op jit(solution)/shard_map/ppermute | solution.py:357
  267.3 60.1 %collective-permute-start.31 = (f32[256,1536]{1,0:T(8,128)}, f32[256,1536]{1,0:T(8,128)}, u32[]{:S(2)}, u32[]{:S(2)}) collective-permute-start(f32[256,1536]{1,0:T(8,128)} %get-tuple-element.60), channel_id=1, source_target_pairs={{0,8},{24,16},{16,24},{8,0},{1,9},{25,17},{17,25},{9,1},{2,10},{26... | collective-permute-start | bytes 4718600 | tf_op jit(solution)/shard_map/ppermute | solution.py:357
  296.9 58.8 %collective-permute-start.32 = (f32[256,1536]{1,0:T(8,128)}, f32[256,1536]{1,0:T(8,128)S(1)}, u32[]{:S(2)}, u32[]{:S(2)}) collective-permute-start(f32[256,1536]{1,0:T(8,128)} %add.49), channel_id=1, source_target_pairs={{8,16},{16,8},{9,17},{17,9},{10,18},{18,10},{11,19},{19,11},{12,20... | collective-permute-start | bytes 4718600 | tf_op jit(solution)/shard_map/ppermute | solution.py:357
  297.9 57.8 %collective-permute-start.33 = (f32[256,1536]{1,0:T(8,128)}, f32[256,1536]{1,0:T(8,128)S(1)}, u32[]{:S(2)}, u32[]{:S(2)}) collective-permute-start(f32[256,1536]{1,0:T(8,128)} %products.15), channel_id=1, source_target_pairs={{0,8},{24,16},{16,24},{8,0},{1,9},{25,17},{17,25},{9,1},{2,10},{26... | collective-permute-start | bytes 4718600 | tf_op jit(solution)/shard_map/ppermute | solution.py:357
  (32 other events, 244.6 us)
Sparse Core Ops, SparseCore 0:
  129.6 44.1 all-gather.8
  175.7 45.5 all-gather.10
  223.1 45.5 all-gather.6

commit v3 on v2

--- a/solution.py
+++ b/solution.py
@@ -15,8 +15,8 @@
 
 CHUNKS = 2
 SHARES = 2
-WORK = 1
-VMEM = 56 * 2**20
+WORK = 0
+VMEM = 60 * 2**20
 f32, bf16 = jnp.float32, jnp.bfloat16
 
 
@@ -48,27 +48,19 @@
     split_ref[0, rows, columns], split_ref[1, rows, columns] = halves(piece)
 
 
-def opening_kernel(parts, share, more, *refs):
-    offsets, pieces, (c_ref, *refs) = refs[0], refs[1 : -3 - 2 * more], refs[-3 - 2 * more :]
-    o_ref, split_ref = refs[-2:]
-    sites = len(pieces) // parts
+def pieces_kernel(sites, parts, share, added, offsets, *refs):
+    (c_ref, *add), (o_ref, split_ref) = refs[-3 - added : -2], refs[-2:]
+    pieces = refs[: -3 - added]
 
     @pl.when((pl.program_id(0) == 0) & (pl.program_id(1) == 0))
     def _():
-        if more:
-            split_ref[...] = refs[1][...]
-        for m in range(sites):
-            for d in range(parts):
-                piece = pieces[m * parts + d][...]
-                row = pl.multiple_of(offsets[m], piece.shape[0])
-                column = pl.multiple_of(offsets[sites + d], piece.shape[1])
-                put(split_ref, piece, row, column)
-
-    products(split_ref, c_ref, refs[0] if more else None, o_ref, share)
-
-
-def split_kernel(added, split_ref, c_ref, *refs):
-    products(split_ref, c_ref, refs[0] if added else None, refs[-1], (0, 1))
+        for p, piece in enumerate(pieces):
+            rows, depth = piece.shape
+            row = pl.multiple_of(offsets[p // parts % sites], rows)
+            column = offsets[sites + p % parts] + p // (sites * parts) * depth
+            put(split_ref, piece[...], row, pl.multiple_of(column, depth))
+
+    products(split_ref, c_ref, add[0] if add else None, o_ref, share)
 
 
 def whole_kernel(added, block_ref, c_ref, *refs):
@@ -78,77 +70,92 @@
     @pl.when(pl.program_id(0) == 0)
     def _():
         for j in range(block_ref.shape[0]):
-            put(split_ref, block_ref[j, k], j * block_ref.shape[2], pl.multiple_of(k * depth, depth))
+            put(split_ref, block_ref[j, 0], j * block_ref.shape[2], pl.multiple_of(k * depth, depth))
 
     products(split_ref, c_ref, refs[0] if added else None, o_ref, (0, 1))
 
 
-def step_kernel(terms, x_ref, y_ref, *refs):
-    coupled = refs[0][...]
-    for term in refs[1:terms]:
-        coupled += term[...]
-    x, y = x_ref[...], y_ref[...]
-    radius = x * x + y * y
-    y_next = y + time_step * (-(kerr_rate * radius - pump_rate + detuning) * x + coupling_gain * coupled)
-    radius_next = x * x + y_next * y_next
-    refs[-2][...] = x + time_step * (kerr_rate * radius_next + pump_rate + detuning) * y_next
-    refs[-1][...] = y_next
-
-
-def oscillate(terms, positions, momenta, lanes, outs):
-    rows, width = positions.shape[0], lanes.stop - lanes.start
-    tile = tile_of(width)
-    there = pl.BlockSpec((rows, tile), lambda i: (0, lanes.start // tile + i))
-    here = pl.BlockSpec((rows, tile), lambda i: (0, i))
-    first = 2 + len(terms)
+def step_kernel(tiles, arrived, x_ref, y_ref, own_ref, *refs):
+    x_out_ref, y_out_ref = refs[-2:]
+    chunk = pl.program_id(0) // tiles
+    for c in range((len(refs) - 2) // arrived):
+
+        @pl.when(chunk == c)
+        def _():
+            coupled = own_ref[...]
+            for term in refs[c * arrived : (c + 1) * arrived]:
+                coupled += term[...]
+            x, y = x_ref[...], y_ref[...]
+            radius = x * x + y * y
+            y_next = y + time_step * (
+                -(kerr_rate * radius - pump_rate + detuning) * x + coupling_gain * coupled
+            )
+            radius_next = x * x + y_next * y_next
+            x_out_ref[...] = x + time_step * (kerr_rate * radius_next + pump_rate + detuning) * y_next
+            y_out_ref[...] = y_next
+
+
+def oscillate(own, arrived, positions, momenta):
+    rows, width = positions.shape
+    chunk = width // len(arrived)
+    tile = tile_of(chunk)
+    tiles = chunk // tile
+    there = pl.BlockSpec((rows, tile), lambda i: (0, i))
+    here = [
+        pl.BlockSpec((rows, tile), lambda i, c=c: (0, jnp.clip(i - c * tiles, 0, tiles - 1)))
+        for c, terms in enumerate(arrived)
+        for _ in terms
+    ]
     return pl.pallas_call(
-        functools.partial(step_kernel, len(terms)),
+        functools.partial(step_kernel, tiles, len(arrived[0])),
         grid=(width // tile,),
-        in_specs=[there, there] + [here] * len(terms) + [pl.BlockSpec(memory_space=pl.ANY)] * len(outs),
+        in_specs=[there] * 3 + here,
         out_specs=[there, there],
         out_shape=[jax.ShapeDtypeStruct(positions.shape, f32)] * 2,
-        input_output_aliases={first + i: i for i in range(len(outs))},
+        compiler_params=pltpu.CompilerParams(vmem_limit_bytes=VMEM),
         name="oscillate",
-    )(positions, momenta, *terms, *outs)
+    )(positions, momenta, own, *[term for terms in arrived for term in terms])
 
 
 def tile_of(width):
     return max(t for t in range(128, 513, 128) if width % t == 0)
 
 
-def call(kernel, operands, couplings, lanes, parts, rows, share=(0, 1), add=(), offsets=None, keep=False):
+def shard_product(shard, couplings, lanes, parts, rows, add=None, offsets=None, share=(0, 1)):
     h, of = share
     start, width = lanes.start, lanes.stop - lanes.start
     depth = couplings.shape[0] // (parts * of)
     tile = tile_of(width)
-
-    def whole(x):
-        return pl.BlockSpec(x.shape, lambda i, k, *_: (0,) * len(x.shape), pipeline_mode=pl.Buffered(1))
-
     result = pl.BlockSpec((rows, tile), lambda i, k, *_: (0, i))
     couple = pl.BlockSpec((depth, tile), lambda i, k, *_: (k * of + h, start // tile + i))
-    in_specs, values = [whole(x) for x in operands] + [couple], [*operands, couplings]
-    in_specs += [result if i == 0 else whole(x) for i, x in enumerate(add)]
-    values += add
-    out_shape, out_specs = [jax.ShapeDtypeStruct((rows, width), f32)], [result]
-    split = jax.ShapeDtypeStruct((2, rows, couplings.shape[0]), bf16)
-    if keep:
-        out_shape.append(split)
-        out_specs.append(pl.BlockSpec(split.shape, lambda i, k, *_: (0, 0, 0)))
-    out = pl.pallas_call(
+    if offsets is not None:
+        values, scalars = list(shard), [offsets]
+        sites = offsets.shape[0] - parts
+        kernel = functools.partial(pieces_kernel, sites, parts, share, int(add is not None))
+        in_specs = [
+            pl.BlockSpec(x.shape, lambda i, k, *_: (0, 0), pipeline_mode=pl.Buffered(1)) for x in values
+        ]
+    else:
+        values, scalars = [shard], []
+        kernel = functools.partial(whole_kernel, add is not None)
+        block = (shard.shape[0], 1, *shard.shape[2:])
+        in_specs = [pl.BlockSpec(block, lambda i, k, *_: (0, jnp.where(i == 0, k, parts - 1), 0, 0))]
+    return pl.pallas_call(
         kernel,
         grid_spec=pltpu.PrefetchScalarGridSpec(
-            num_scalar_prefetch=int(offsets is not None),
+            num_scalar_prefetch=len(scalars),
             grid=(width // tile, parts),
-            in_specs=in_specs,
-            out_specs=out_specs,
+            in_specs=in_specs + [couple] + ([] if add is None else [result]),
+            out_specs=result,
+            scratch_shapes=[pltpu.VMEM((2, rows, couplings.shape[0]), bf16)],
         ),
-        out_shape=out_shape,
+        out_shape=jax.ShapeDtypeStruct((rows, width), f32),
         compiler_params=pltpu.CompilerParams(vmem_limit_bytes=VMEM),
-        cost_estimate=pl.CostEstimate(flops=WORK * rows * width * depth * parts, bytes_accessed=0, transcendentals=0),
+        cost_estimate=pl.CostEstimate(
+            flops=WORK * rows * width * depth * parts, bytes_accessed=0, transcendentals=0
+        ),
         name="products",
-    )(*(() if offsets is None else (offsets,)), *values)
-    return out if keep else out[0]
+    )(*scalars, *values, couplings, *([] if add is None else [add]))
 
 
 def after(x, *others):
@@ -302,64 +309,63 @@
     for h in range(SHARES):
         own.append(exchange_rows(plan, 0, spread[h], row, col, *own[-1:]))
     opening = [gather_sites(plan, part) for part in own]
+    second = []
+    for h in range(SHARES):
+        second.append(exchange_rows(plan, 1, spread[h], row, col, own[-1]))
     spread = [jnp.concatenate(share, axis=1) for share in zip(*spread)]
-    for k in range(1, n):
-        own.append(exchange_rows(plan, k, spread, row, col, *own[SHARES - 1 :][: 1 if k < n - 1 else None]))
-    own = own[SHARES - 1 :]
+    shares = [None, second[-1]]
+    for k in range(2, n):
+        before = own[-1:] if k < n - 1 else [shares[-1]]
+        shares.append(exchange_rows(plan, k, spread, row, col, *before))
 
     partial = [[None] * CHUNKS for _ in range(n)]
     sums = [[Sums() for _ in range(CHUNKS)] for _ in range(n)]
-    rows, so_far, outs = positions.shape[0], None, []
+    rows = positions.shape[0]
+    first, pieces = None, []
     for h in range(SHARES):
-        pieces = opening[h]
+        part = opening[h]
         if h:
-            couplings = after(couplings, so_far[0], own[SHARES])
-            pieces = [after(piece, so_far[0]) for piece in pieces]
-        pieces = gather_parts(plan, pieces)
-        so_far = call(
-            functools.partial(opening_kernel, plan.ratio, (h, SHARES), so_far is not None),
-            pieces,
+            couplings = after(couplings, first, shares[2], *second[:-1])
+            part = [after(piece, first) for piece in part]
+        part = gather_parts(plan, part)
+        pieces += part
+        first = shard_product(
+            part,
             couplings,
             lanes[0],
             plan.ratio,
             rows,
+            add=first,
+            offsets=piece_offsets(plan, rows // n, width, h * depth, col),
             share=(h, SHARES),
-            add=so_far or (),
-            offsets=piece_offsets(plan, rows // n, width, h * depth, col),
-            keep=True,
         )
-    partial[0][0], block = so_far
-    own = [after(part, partial[0][0], own[-2]) for part in own]
-    gathered = [None] + [gather_plane(plan, part) for part in own[1:]]
-    couplings = after(couplings, *own[1:])
-    last = partial[0][0]
+    partial[0][0] = last = first
+    shares[1] = jnp.concatenate([after(part, first) for part in second], axis=1)
+    shards = [pieces] + [gather_plane(plan, after(part, first, shares[-2])) for part in shares[1:]]
+    couplings = after(couplings, *shares[1:])
     for t in range(n):
-        for c, span in enumerate(lanes):
-            add = []
+        for c, span in enumerate(lanes if t < n - 1 else [slice(0, width)]):
+            add = None
             if 0 < t < n - 1:
-                add = [sums[t - 1][c].carried(plan.sources(t, t), row)]
+                add = sums[t - 1][c].carried(plan.sources(t, t), row)
             if t or c:
                 before = [array for array, _ in sums[t - 1][c].arrays] if 0 < t < n - 1 else []
-                couplings = after(couplings, last, *before)
-                first = c == 0 and t > 0
-                operand = gathered[t] if first else block
-                kernel = functools.partial(whole_kernel if first else split_kernel, len(add))
-                out = call(kernel, [operand], couplings, span, plan.ratio, rows, add=add, keep=first)
-                last, block = out if first else (out, block)
+                couplings = after(couplings, last, *sent, *before)
+                offsets = None if t else piece_offsets(plan, rows // n, width, 0, col)
+                last = shard_product(shards[t], couplings, span, plan.ratio, rows, add=add, offsets=offsets)
                 partial[t][c] = last
+            sent = []
             for k in range(t + 1):
                 mine = partial[t][c]
                 if k < t:
                     if not plan.messages(t, k):
                         continue
                     mine = after(partial[k][c], partial[t][c]) + sums[t - 1][c].carried(plan.sources(t, k), row)
+                sent.append(mine)
                 for pairs in plan.messages(t, k):
                     sums[t][c].add(lax.ppermute(mine, "row", pairs), pairs)
-            if t == n - 1:
-                terms = [last] + [array for array, _ in sums[n - 2][c].arrays]
-                outs = oscillate(terms, positions, momenta, span, outs)
-                couplings = after(couplings, outs[0])
-    return outs
+    arrived = [[array for array, _ in sums[n - 2][c].arrays] for c in range(CHUNKS)]
+    return oscillate(last, arrived, positions, momenta)
 
 
 def solution(mesh):

time: 371 us -> 360 us (0.970)
  Pallas kernels: 214 us -> 194 us
  local copies, waits for them, and re-layouts: 5.59 us -> 10.5 us
    pallas_call x11 -> x9, Pallas kernels: 214 us -> 194 us  [the longest x8 184 us: shard_product(): pl.pallas_call(kernel, grid_spec=pltpu.PrefetchScalarGridSpec(num_scalar_...]
    ppermute x4 -> x5, waiting for transfers between devices: 16.1 us -> 9.41 us  [exchange_rows(): lax.ppermute(part, 'row', pairs)]
    ppermute x6, waiting for transfers between devices: 5.25 us -> 11.4 us  [gather_sites(): lax.ppermute(part, 'col', plan.site_pairs(m))]
    unnamed x38 -> x47, local copies, waits for them, and re-layouts: 2.8 us -> 6.87 us
    select_n x3 -> x5, other arithmetic: 5.76 us -> 9.15 us  [one_of(): out = jnp.where(index == i, values[i], out)]
    ppermute x4 -> x5, starting transfers between devices: 10.1 us -> 11.1 us  [exchange_rows(): lax.ppermute(part, 'row', pairs)]
  transfers between devices with their start and end apart: 37 -> 38, of which waited for: 13 -> 15; matrix products, arithmetic and copies ran while one was open for 2% -> 3% of each run, Pallas kernels for 56% -> 51%
where the time goes in v3:
time: 360 us; the launch traced here: 358 us
  Pallas kernels  194 us (54%)
  waiting for transfers between devices  70.8 us (20%)
  starting transfers between devices  56 us (16%)
  between operations  14.1 us (4%)
  other arithmetic  13.2 us (4%)
  local copies, waits for them, and re-layouts  10.5 us (3%)
    pallas_call x8, Pallas kernels, shard_product(): pl.pallas_call(kernel, grid_spec=pltpu.PrefetchScalarGridSpec(num_scalar_...  184 us
    ppermute x10, starting transfers between devices, per_device(): sums[t][c].add(lax.ppermute(mine, 'row', pairs), pairs)  28.8 us
    ppermute x6, waiting for transfers between devices, spread_sites(): lax.ppermute(part, 'col', plan.site_pairs(m))  26.1 us
    ppermute x10, waiting for transfers between devices, per_device(): sums[t][c].add(lax.ppermute(mine, 'row', pairs), pairs)  15.3 us
    ppermute x6, waiting for transfers between devices, gather_sites(): lax.ppermute(part, 'col', plan.site_pairs(m))  11.4 us
    ppermute x5, starting transfers between devices, exchange_rows(): lax.ppermute(part, 'row', pairs)  11.1 us
    pallas_call x1, Pallas kernels, oscillate(): pl.pallas_call(functools.partial(step_kernel, tiles, len(arrived[0])), gr...  9.95 us
    ppermute x5, waiting for transfers between devices, exchange_rows(): lax.ppermute(part, 'row', pairs)  9.41 us
  transfers between devices with their start and end apart: 38, of which 15 were waited for; matrix products, arithmetic and copies ran while one was open for 3% of the time, Pallas kernels for 51%

profile of v3, /device:TPU:0, one launch (start us, length us, event | category | flops | bytes accessed | tf_op | source)
XLA Modules:
  0.0 358.4 jit_solution(8590594533233276099)
XLA Ops:
  8.6 4.0 %collective-permute-start = (f32[64,1536]{1,0:T(8,128)S(1)}, f32[64,1536]{1,0:T(8,128)S(1)}, u32[]{:S(2)}, u32[]{:S(2)}) collective-permute-start(f32[64,1536]{1,0:T(8,128)S(1)} %get-tuple-element.61), channel_id=1, source_target_pairs={{0,6},{1,7},{2,4},{3,5},{4,2},{5,3},{6,0},{7,1},{8,14},{9,15},{10,... | collective-permute-start | bytes 1179656 | tf_op jit(solution)/shard_map/ppermute | solution.py:238
  13.2 9.3 %collective-permute-done = f32[64,1536]{1,0:T(8,128)S(1)} collective-permute-done((f32[64,1536]{1,0:T(8,128)S(1)}, f32[64,1536]{1,0:T(8,128)S(1)}, u32[]{:S(2)}, u32[]{:S(2)}) %collective-permute-start) | collective-permute-done | bytes 393248 | tf_op jit(solution)/shard_map/ppermute | solution.py:238
  22.5 7.6 %collective-permute-done.2 = f32[64,1536]{1,0:T(8,128)S(1)} collective-permute-done((f32[64,1536]{1,0:T(8,128)S(1)}, f32[64,1536]{1,0:T(8,128)S(1)}, u32[]{:S(2)}, u32[]{:S(2)}) %collective-permute-start.2) | collective-permute-done | bytes 393248 | tf_op jit(solution)/shard_map/ppermute | solution.py:238
  35.0 3.6 %collective-permute-start.6 = (f32[64,1536]{1,0:T(8,128)}, f32[64,1536]{1,0:T(8,128)S(1)}, u32[]{:S(2)}, u32[]{:S(2)}) collective-permute-start(f32[64,1536]{1,0:T(8,128)} %get-tuple-element.62), channel_id=1, source_target_pairs={{0,24},{8,16},{16,8},{24,0},{1,25},{9,17},{17,9},{25,1},{2,26},{10... | collective-permute-start | bytes 1179656 | tf_op jit(solution)/shard_map/ppermute | solution.py:249
  42.1 6.0 %collective-permute-done.6.refs_0_ = f32[64,1536]{1,0:T(8,128)S(1)} collective-permute-done((f32[64,1536]{1,0:T(8,128)}, f32[64,1536]{1,0:T(8,128)S(1)}, u32[]{:S(2)}, u32[]{:S(2)}) %collective-permute-start.6) | collective-permute-done | bytes 393248 | tf_op jit(solution)/shard_map/ppermute | solution.py:249
  53.4 5.5 %collective-permute-done.3 = f32[64,1536]{1,0:T(8,128)} collective-permute-done((f32[64,1536]{1,0:T(8,128)}, f32[64,1536]{1,0:T(8,128)}, u32[]{:S(2)}, u32[]{:S(2)}) %collective-permute-start.3) | collective-permute-done | bytes 393248 | tf_op jit(solution)/shard_map/ppermute | solution.py:238
  63.7 4.8 %collective-permute-done.10.refs_2_ = f32[64,1536]{1,0:T(8,128)S(1)} collective-permute-done((f32[64,1536]{1,0:T(8,128)S(1)}, f32[64,1536]{1,0:T(8,128)S(1)}, u32[]{:S(2)}, u32[]{:S(2)}) %collective-permute-start.10) | collective-permute-done | bytes 393248 | tf_op jit(solution)/shard_map/ppermute | solution.py:258
  69.1 6.6 %collective-permute-done.14.refs_6_ = f32[64,1536]{1,0:T(8,128)S(1)} collective-permute-done((f32[64,1536]{1,0:T(8,128)S(1)}, f32[64,1536]{1,0:T(8,128)S(1)}, u32[]{:S(2)}, u32[]{:S(2)}) %collective-permute-start.14) | collective-permute-done | bytes 393248 | tf_op jit(solution)/shard_map/ppermute | solution.py:258
  77.0 4.1 %collective-permute-start.8 = (f32[64,3072]{1,0:T(8,128)}, f32[64,3072]{1,0:T(8,128)S(1)}, u32[]{:S(2)}, u32[]{:S(2)}) collective-permute-start(f32[64,3072]{1,0:T(8,128)} %get-tuple-element.27), channel_id=1, source_target_pairs={{0,8},{8,0},{16,24},{24,16},{1,9},{9,1},{17,25},{25,17},{2,10},{10... | collective-permute-start | bytes 2359304 | tf_op jit(solution)/shard_map/ppermute | solution.py:249
  86.7 14.9 %products.8.refs_9_ = f32[256,1536]{1,0:T(8,128)} custom-call(s32[6]{0:T(128)} %stack.50.offsets, f32[64,1536]{1,0:T(8,128)} %copy-done.3, f32[64,1536]{1,0:T(8,128)} %copy-done.7, f32[64,1536]{1,0:T(8,128)} %copy-done.4, f32[64,1536]{1,0:T(8,128)} %copy-done.8, f32[64,1536]{1,0:T(8,128)} %copy-done.5, f32[64,1536]{1,0:T(8,128)} %copy-done.9, ...), custom_call_target="tpu_custom_call" | custom-call | tf_op jit(solution)/shard_map/products/pallas_call | solution.py:143
  110.6 15.4 %products.9 = f32[256,1536]{1,0:T(8,128)} custom-call(s32[6]{0:T(128)} %stack.47.offsets, f32[64,1536]{1,0:T(8,128)} %collective-permute-done.7.refs_0_.refs_8_, f32[64,1536]{1,0:T(8,128)} %copy-done.14, f32[64,1536]{1,0:T(8,128)} %copy-done.11, f32[64,1536]{1,0:T(8,128)} %copy-done.15, f32[64,1536]{1,0:T(8,128)} %copy-done.12, f32[64,1536]{1,0:T(8,128)} %copy-done.16, ...), custom_call_target="tpu_custom_call" | custom-call | tf_op jit(solution)/shard_map/products/pallas_call | solution.py:143
  133.2 24.8 %products.10 = f32[256,1536]{1,0:T(8,128)} custom-call(s32[6]{0:T(128)} %stack.50.offsets, f32[64,1536]{1,0:T(8,128)} %copy-done.3, f32[64,1536]{1,0:T(8,128)} %copy-done.7, f32[64,1536]{1,0:T(8,128)} %copy-done.4, f32[64,1536]{1,0:T(8,128)} %copy-done.8, f32[64,1536]{1,0:T(8,128)} %copy-done.5, f32[64,1536]{1,0:T(8,128)} %copy-done.9, ...), custom_call_target="tpu_custom_call" | custom-call | tf_op jit(solution)/shard_map/products/pallas_call | solution.py:143
  160.4 7.4 %collective-permute-done.25.refs_0_ = f32[256,1536]{1,0:T(8,128)S(1)} collective-permute-done((f32[256,1536]{1,0:T(8,128)S(1)}, f32[256,1536]{1,0:T(8,128)S(1)}, u32[]{:S(2)}, u32[]{:S(2)}) %collective-permute-start.25) | collective-permute-done | bytes 1572896 | tf_op jit(solution)/shard_map/ppermute | solution.py:366
  167.8 7.1 %all-gather.9.cloned.1.call-done = f32[512,3072]{1,0:T(8,128)} async-done(((f32[64,3072]{1,0:T(8,128)}), f32[512,3072]{1,0:T(8,128)}) %all-gather.9.cloned.1.call-update) | async-done | bytes 6291472 | tf_op jit(solution)/shard_map/all_gather | solution.py:253
  174.9 22.4 %products.11 = f32[256,1536]{1,0:T(8,128)} custom-call(f32[4,2,64,3072]{3,2,1,0:T(8,128)} %bitcast.13, f32[6144,3072]{1,0:T(8,128)} %c_ref.4, f32[256,1536]{1,0:T(8,128)} %copy-done.21), custom_call_target="tpu_custom_call" | custom-call | tf_op jit(solution)/shard_map/products/pallas_call | solution.py:143
  197.3 4.6 %collective-permute-start.27 = (f32[256,1536]{1,0:T(8,128)}, f32[256,1536]{1,0:T(8,128)}, u32[]{:S(2)}, u32[]{:S(2)}) collective-permute-start(f32[256,1536]{1,0:T(8,128)} %products.11), channel_id=1, source_target_pairs={{0,8},{24,16},{1,9},{25,17},{2,10},{26,18},{3,11},{27,19},{4,12},{... | collective-permute-start | bytes 4718600 | tf_op jit(solution)/shard_map/ppermute | solution.py:366
  203.9 22.4 %products.12 = f32[256,1536]{1,0:T(8,128)} custom-call(f32[4,2,64,3072]{3,2,1,0:T(8,128)} %bitcast.14, f32[6144,3072]{1,0:T(8,128)} %c_ref.4, f32[256,1536]{1,0:T(8,128)} %collective-permute-done.26.refs_0_), custom_call_target="tpu_custom_call" | custom-call | tf_op jit(solution)/shard_map/products/pallas_call | solution.py:143
  229.9 6.0 %collective-permute-done.27 = f32[256,1536]{1,0:T(8,128)} collective-permute-done((f32[256,1536]{1,0:T(8,128)}, f32[256,1536]{1,0:T(8,128)}, u32[]{:S(2)}, u32[]{:S(2)}) %collective-permute-start.27) | collective-permute-done | bytes 1572896 | tf_op jit(solution)/shard_map/ppermute | solution.py:366
  235.8 22.5 %products.13 = f32[256,1536]{1,0:T(8,128)} custom-call(f32[4,2,64,3072]{3,2,1,0:T(8,128)} %bitcast.11, f32[6144,3072]{1,0:T(8,128)} %c_ref.4, f32[256,1536]{1,0:T(8,128)} %collective-permute-done.28.refs_0_), custom_call_target="tpu_custom_call" | custom-call | tf_op jit(solution)/shard_map/products/pallas_call | solution.py:143
  258.3 4.6 %collective-permute-start.32 = (f32[256,1536]{1,0:T(8,128)}, f32[256,1536]{1,0:T(8,128)}, u32[]{:S(2)}, u32[]{:S(2)}) collective-permute-start(f32[256,1536]{1,0:T(8,128)} %products.13), channel_id=1, source_target_pairs={{0,8},{24,16},{16,24},{8,0},{1,9},{25,17},{17,25},{9,1},{2,10},{26... | collective-permute-start | bytes 4718600 | tf_op jit(solution)/shard_map/ppermute | solution.py:366
  269.5 22.3 %products.14 = f32[256,1536]{1,0:T(8,128)} custom-call(f32[4,2,64,3072]{3,2,1,0:T(8,128)} %bitcast.12, f32[6144,3072]{1,0:T(8,128)} %c_ref.4, f32[256,1536]{1,0:T(8,128)} %collective-permute-done.30.refs_0_), custom_call_target="tpu_custom_call" | custom-call | tf_op jit(solution)/shard_map/products/pallas_call | solution.py:143
  293.9 6.5 %collective-permute-start.34 = (f32[256,1536]{1,0:T(8,128)}, f32[256,1536]{1,0:T(8,128)S(1)}, u32[]{:S(2)}, u32[]{:S(2)}) collective-permute-start(f32[256,1536]{1,0:T(8,128)} %products.14), channel_id=1, source_target_pairs={{0,8},{24,16},{16,24},{8,0},{1,9},{25,17},{17,25},{9,1},{2,10},{26... | collective-permute-start | bytes 4718600 | tf_op jit(solution)/shard_map/ppermute | solution.py:366
  300.4 39.1 %products.15.own_ref = f32[256,3072]{1,0:T(8,128)} custom-call(f32[4,2,64,3072]{3,2,1,0:T(8,128)} %bitcast.15, f32[6144,3072]{1,0:T(8,128)} %c_ref.4), custom_call_target="tpu_custom_call" | custom-call | tf_op jit(solution)/shard_map/products/pallas_call | solution.py:143
  341.9 10.0 %oscillate.1 = (f32[256,3072]{1,0:T(8,128)}, f32[256,3072]{1,0:T(8,128)}) custom-call(f32[256,3072]{1,0:T(8,128)} %x_ref.1, f32[256,3072]{1,0:T(8,128)} %y_ref.1, f32[256,3072]{1,0:T(8,128)} %products.15.own_ref, f32[256,1536]{1,0:T(8,128)} %collective-permute-done.31.refs_0_, f32[256,1536]{1,0:T(8,128)} %collective-permute-done.32.refs_1_, ...), custom_call_target="tpu_custom_call" | custom-call | tf_op jit(solution)/shard_map/oscillate/pallas_call | solution.py:109
  (122 shorter events, 62.9 us)
Async XLA Ops:
  7.2 167.8 %all-gather.9.cloned.1.call-start = ((), (), s32[]{:S(2)}) async-start(), calls=%async_computation.1 | async-start | bytes 7077888 | tf_op jit(solution)/shard_map/all_gather | solution.py:253
  40.2 18.7 %collective-permute-start.3 = (f32[64,1536]{1,0:T(8,128)}, f32[64,1536]{1,0:T(8,128)}, u32[]{:S(2)}, u32[]{:S(2)}) collective-permute-start(f32[64,1536]{1,0:T(8,128)} %get-tuple-element.57), channel_id=1, source_target_pairs={{0,4},{1,5},{2,6},{3,7},{4,0},{5,1},{6,2},{7,3},{8,12},{9,13},{10,... | collective-permute-start | bytes 1179656 | tf_op jit(solution)/shard_map/ppermute | solution.py:238
  41.5 18.7 %collective-permute-start.5 = (f32[64,1536]{1,0:T(8,128)}, f32[64,1536]{1,0:T(8,128)}, u32[]{:S(2)}, u32[]{:S(2)}) collective-permute-start(f32[64,1536]{1,0:T(8,128)} %get-tuple-element.56), channel_id=1, source_target_pairs={{0,2},{1,3},{2,0},{3,1},{4,6},{5,7},{6,4},{7,5},{8,10},{9,11},{10,... | collective-permute-start | bytes 1179656 | tf_op jit(solution)/shard_map/ppermute | solution.py:238
  48.1 20.5 %collective-permute-start.10 = (f32[64,1536]{1,0:T(8,128)S(1)}, f32[64,1536]{1,0:T(8,128)S(1)}, u32[]{:S(2)}, u32[]{:S(2)}) collective-permute-start(f32[64,1536]{1,0:T(8,128)S(1)} %collective-permute-done.6.refs_0_), channel_id=1, source_target_pairs={{0,2},{1,3},{2,0},{3,1},{4,6},{5,7},{6,4},{7,5},{8,10},{9,11},{10,... | collective-permute-start | bytes 1179656 | tf_op jit(solution)/shard_map/ppermute | solution.py:258
  49.6 19.0 %collective-permute-start.12 = (f32[64,1536]{1,0:T(8,128)S(1)}, f32[64,1536]{1,0:T(8,128)S(1)}, u32[]{:S(2)}, u32[]{:S(2)}) collective-permute-start(f32[64,1536]{1,0:T(8,128)S(1)} %collective-permute-done.6.refs_0_), channel_id=1, source_target_pairs={{0,4},{1,5},{2,6},{3,7},{4,0},{5,1},{6,2},{7,3},{8,12},{9,13},{10,... | collective-permute-start | bytes 1179656 | tf_op jit(solution)/shard_map/ppermute | solution.py:258
  51.8 23.9 %collective-permute-start.14 = (f32[64,1536]{1,0:T(8,128)S(1)}, f32[64,1536]{1,0:T(8,128)S(1)}, u32[]{:S(2)}, u32[]{:S(2)}) collective-permute-start(f32[64,1536]{1,0:T(8,128)S(1)} %collective-permute-done.6.refs_0_), channel_id=1, source_target_pairs={{0,6},{1,7},{2,4},{3,5},{4,2},{5,3},{6,0},{7,1},{8,14},{9,15},{10,... | collective-permute-start | bytes 1179656 | tf_op jit(solution)/shard_map/ppermute | solution.py:258
  77.0 28.7 %collective-permute-start.8 = (f32[64,3072]{1,0:T(8,128)}, f32[64,3072]{1,0:T(8,128)S(1)}, u32[]{:S(2)}, u32[]{:S(2)}) collective-permute-start(f32[64,3072]{1,0:T(8,128)} %get-tuple-element.27), channel_id=1, source_target_pairs={{0,8},{8,0},{16,24},{24,16},{1,9},{9,1},{17,25},{25,17},{2,10},{10... | collective-permute-start | bytes 2359304 | tf_op jit(solution)/shard_map/ppermute | solution.py:249
  81.2 20.5 %collective-permute-start.17 = (f32[64,1536]{1,0:T(8,128)}, f32[64,1536]{1,0:T(8,128)S(1)}, u32[]{:S(2)}, u32[]{:S(2)}) collective-permute-start(f32[64,1536]{1,0:T(8,128)} %collective-permute-done.7.refs_0_.refs_8_), channel_id=1, source_target_pairs={{0,2},{1,3},{2,0},{3,1},{4,6},{5,7},{6,4},{7,5},{8,10},{9,11},{10,... | collective-permute-start | bytes 1179656 | tf_op jit(solution)/shard_map/ppermute | solution.py:258
  82.8 18.9 %collective-permute-start.19 = (f32[64,1536]{1,0:T(8,128)}, f32[64,1536]{1,0:T(8,128)S(1)}, u32[]{:S(2)}, u32[]{:S(2)}) collective-permute-start(f32[64,1536]{1,0:T(8,128)} %collective-permute-done.7.refs_0_.refs_8_), channel_id=1, source_target_pairs={{0,4},{1,5},{2,6},{3,7},{4,0},{5,1},{6,2},{7,3},{8,12},{9,13},{10,... | collective-permute-start | bytes 1179656 | tf_op jit(solution)/shard_map/ppermute | solution.py:258
  82.9 19.3 %collective-permute-start.21 = (f32[64,1536]{1,0:T(8,128)}, f32[64,1536]{1,0:T(8,128)S(1)}, u32[]{:S(2)}, u32[]{:S(2)}) collective-permute-start(f32[64,1536]{1,0:T(8,128)} %collective-permute-done.7.refs_0_.refs_8_), channel_id=1, source_target_pairs={{0,6},{1,7},{2,4},{3,5},{4,2},{5,3},{6,0},{7,1},{8,14},{9,15},{10,... | collective-permute-start | bytes 1179656 | tf_op jit(solution)/shard_map/ppermute | solution.py:258
  85.5 19.3 %collective-permute-start.23 = (f32[64,1536]{1,0:T(8,128)}, f32[64,1536]{1,0:T(8,128)}, u32[]{:S(2)}, u32[]{:S(2)}) collective-permute-start(f32[64,1536]{1,0:T(8,128)} %get-tuple-element.33), channel_id=1, source_target_pairs={{0,16},{8,24},{16,0},{24,8},{1,17},{9,25},{17,1},{25,9},{2,18},{10... | collective-permute-start | bytes 1179656 | tf_op jit(solution)/shard_map/ppermute | solution.py:249
  105.7 21.3 %collective-permute-start.24 = (f32[64,1536]{1,0:T(8,128)}, f32[64,1536]{1,0:T(8,128)}, u32[]{:S(2)}, u32[]{:S(2)}) collective-permute-start(f32[64,1536]{1,0:T(8,128)} %get-tuple-element.37), channel_id=1, source_target_pairs={{0,16},{8,24},{16,0},{24,8},{1,17},{9,25},{17,1},{25,9},{2,18},{10... | collective-permute-start | bytes 1179656 | tf_op jit(solution)/shard_map/ppermute | solution.py:249
  129.1 106.7 %all-gather.11.cloned.1.call-start = ((), (), s32[]{:S(2)}) async-start(), calls=%async_computation.2 | async-start | bytes 7077888 | tf_op jit(solution)/shard_map/all_gather | solution.py:253
  129.9 170.5 %all-gather.7.cloned.1.call-start = ((), (), s32[]{:S(2)}) async-start(), calls=%async_computation | async-start | bytes 7077888 | tf_op jit(solution)/shard_map/all_gather | solution.py:253
  130.6 37.2 %collective-permute-start.25 = (f32[256,1536]{1,0:T(8,128)S(1)}, f32[256,1536]{1,0:T(8,128)S(1)}, u32[]{:S(2)}, u32[]{:S(2)}) collective-permute-start(f32[256,1536]{1,0:T(8,128)S(1)} %copy-done), channel_id=1, source_target_pairs={{0,8},{24,16},{1,9},{25,17},{2,10},{26,18},{3,11},{27,19},{4,12},{... | collective-permute-start | bytes 4718600 | tf_op jit(solution)/shard_map/ppermute | solution.py:366
  158.0 45.9 %collective-permute-start.26 = (f32[256,1536]{1,0:T(8,128)}, f32[256,1536]{1,0:T(8,128)}, u32[]{:S(2)}, u32[]{:S(2)}) collective-permute-start(f32[256,1536]{1,0:T(8,128)} %products.10), channel_id=1, source_target_pairs={{0,8},{24,16},{1,9},{25,17},{2,10},{26,18},{3,11},{27,19},{4,12},{... | collective-permute-start | bytes 4718600 | tf_op jit(solution)/shard_map/ppermute | solution.py:366
  197.3 38.5 %collective-permute-start.27 = (f32[256,1536]{1,0:T(8,128)}, f32[256,1536]{1,0:T(8,128)}, u32[]{:S(2)}, u32[]{:S(2)}) collective-permute-start(f32[256,1536]{1,0:T(8,128)} %products.11), channel_id=1, source_target_pairs={{0,8},{24,16},{1,9},{25,17},{2,10},{26,18},{3,11},{27,19},{4,12},{... | collective-permute-start | bytes 4718600 | tf_op jit(solution)/shard_map/ppermute | solution.py:366
  202.0 33.9 %collective-permute-start.28 = (f32[256,1536]{1,0:T(8,128)}, f32[256,1536]{1,0:T(8,128)}, u32[]{:S(2)}, u32[]{:S(2)}) collective-permute-start(f32[256,1536]{1,0:T(8,128)} %products.11), channel_id=1, source_target_pairs={{8,16},{16,8},{9,17},{17,9},{10,18},{18,10},{11,19},{19,11},{12,20... | collective-permute-start | bytes 4718600 | tf_op jit(solution)/shard_map/ppermute | solution.py:366
  226.3 43.3 %collective-permute-start.29 = (f32[256,1536]{1,0:T(8,128)}, f32[256,1536]{1,0:T(8,128)S(1)}, u32[]{:S(2)}, u32[]{:S(2)}) collective-permute-start(f32[256,1536]{1,0:T(8,128)} %products.12), channel_id=1, source_target_pairs={{0,8},{24,16},{1,9},{25,17},{2,10},{26,18},{3,11},{27,19},{4,12},{... | collective-permute-start | bytes 4718600 | tf_op jit(solution)/shard_map/ppermute | solution.py:366
  228.0 41.5 %collective-permute-start.30 = (f32[256,1536]{1,0:T(8,128)}, f32[256,1536]{1,0:T(8,128)}, u32[]{:S(2)}, u32[]{:S(2)}) collective-permute-start(f32[256,1536]{1,0:T(8,128)} %products.12), channel_id=1, source_target_pairs={{8,16},{16,8},{9,17},{17,9},{10,18},{18,10},{11,19},{19,11},{12,20... | collective-permute-start | bytes 4718600 | tf_op jit(solution)/shard_map/ppermute | solution.py:366
  258.3 81.2 %collective-permute-start.32 = (f32[256,1536]{1,0:T(8,128)}, f32[256,1536]{1,0:T(8,128)}, u32[]{:S(2)}, u32[]{:S(2)}) collective-permute-start(f32[256,1536]{1,0:T(8,128)} %products.13), channel_id=1, source_target_pairs={{0,8},{24,16},{16,24},{8,0},{1,9},{25,17},{17,25},{9,1},{2,10},{26... | collective-permute-start | bytes 4718600 | tf_op jit(solution)/shard_map/ppermute | solution.py:366
  265.6 73.8 %collective-permute-start.31 = (f32[256,1536]{1,0:T(8,128)}, f32[256,1536]{1,0:T(8,128)}, u32[]{:S(2)}, u32[]{:S(2)}) collective-permute-start(f32[256,1536]{1,0:T(8,128)} %add.50), channel_id=1, source_target_pairs={{8,16},{16,8},{9,17},{17,9},{10,18},{18,10},{11,19},{19,11},{12,20... | collective-permute-start | bytes 4718600 | tf_op jit(solution)/shard_map/ppermute | solution.py:366
  293.2 46.3 %collective-permute-start.33 = (f32[256,1536]{1,0:T(8,128)}, f32[256,1536]{1,0:T(8,128)S(1)}, u32[]{:S(2)}, u32[]{:S(2)}) collective-permute-start(f32[256,1536]{1,0:T(8,128)} %add.51), channel_id=1, source_target_pairs={{8,16},{16,8},{9,17},{17,9},{10,18},{18,10},{11,19},{19,11},{12,20... | collective-permute-start | bytes 4718600 | tf_op jit(solution)/shard_map/ppermute | solution.py:366
  293.9 45.6 %collective-permute-start.34 = (f32[256,1536]{1,0:T(8,128)}, f32[256,1536]{1,0:T(8,128)S(1)}, u32[]{:S(2)}, u32[]{:S(2)}) collective-permute-start(f32[256,1536]{1,0:T(8,128)} %products.14), channel_id=1, source_target_pairs={{0,8},{24,16},{16,24},{8,0},{1,9},{25,17},{17,25},{9,1},{2,10},{26... | collective-permute-start | bytes 4718600 | tf_op jit(solution)/shard_map/ppermute | solution.py:366
  (37 other events, 298.1 us)
Sparse Core Ops, SparseCore 0:
  129.2 45.6 all-gather.8
  176.8 45.5 all-gather.10
  224.2 45.5 all-gather.6

commit v4 on v3

--- a/solution.py
+++ b/solution.py
@@ -57,7 +57,7 @@
         for p, piece in enumerate(pieces):
             rows, depth = piece.shape
             row = pl.multiple_of(offsets[p // parts % sites], rows)
-            column = offsets[sites + p % parts] + p // (sites * parts) * depth
+            column = offsets[sites + p % parts] + (share[0] + p // (sites * parts)) * depth
             put(split_ref, piece[...], row, pl.multiple_of(column, depth))
 
     products(split_ref, c_ref, add[0] if add else None, o_ref, share)
@@ -98,7 +98,7 @@
 def oscillate(own, arrived, positions, momenta):
     rows, width = positions.shape
     chunk = width // len(arrived)
-    tile = tile_of(chunk)
+    tile = tile_of(chunk, 256)
     tiles = chunk // tile
     there = pl.BlockSpec((rows, tile), lambda i: (0, i))
     here = [
@@ -117,8 +117,8 @@
     )(positions, momenta, own, *[term for terms in arrived for term in terms])
 
 
-def tile_of(width):
-    return max(t for t in range(128, 513, 128) if width % t == 0)
+def tile_of(width, most=512):
+    return max(t for t in range(128, most + 1, 128) if width % t == 0)
 
 
 def shard_product(shard, couplings, lanes, parts, rows, add=None, offsets=None, share=(0, 1)):
@@ -264,11 +264,11 @@
     return [p if d == 0 else lax.ppermute(p, "col", turns[d]) for p in pieces for d in range(r)]
 
 
-def piece_offsets(plan, rows, depth, start, col):
+def piece_offsets(plan, rows, depth, col):
     n, r = plan.n, plan.ratio
     site, part = col // r, lax.rem(col, r)
     starts = [unshift(plan, site, m) * rows for m in range(n)]
-    starts += [lax.rem(part - d + r, r) * depth + start for d in range(r)]
+    starts += [lax.rem(part - d + r, r) * depth for d in range(r)]
     return jnp.stack(starts).astype(jnp.int32)
 
 
@@ -321,7 +321,7 @@
     partial = [[None] * CHUNKS for _ in range(n)]
     sums = [[Sums() for _ in range(CHUNKS)] for _ in range(n)]
     rows = positions.shape[0]
-    first, pieces = None, []
+    first, pieces, offsets = None, [], piece_offsets(plan, rows // n, width, col)
     for h in range(SHARES):
         part = opening[h]
         if h:
@@ -336,7 +336,7 @@
             plan.ratio,
             rows,
             add=first,
-            offsets=piece_offsets(plan, rows // n, width, h * depth, col),
+            offsets=offsets,
             share=(h, SHARES),
         )
     partial[0][0] = last = first
@@ -351,8 +351,7 @@
             if t or c:
                 before = [array for array, _ in sums[t - 1][c].arrays] if 0 < t < n - 1 else []
                 couplings = after(couplings, last, *sent, *before)
-                offsets = None if t else piece_offsets(plan, rows // n, width, 0, col)
-                last = shard_product(shards[t], couplings, span, plan.ratio, rows, add=add, offsets=offsets)
+                last = shard_product(shards[t], couplings, span, plan.ratio, rows, add, None if t else offsets)
                 partial[t][c] = last
             sent = []
             for k in range(t + 1):

time: 360 us -> 361 us (level)
  transfers between devices with their start and end apart: 38 -> 38, of which waited for: 15 -> 16; matrix products, arithmetic and copies ran while one was open for 3% -> 3% of each run, Pallas kernels for 51% -> 51%
where the time goes in v4:
time: 361 us; the launch traced here: 359 us
  Pallas kernels  196 us (54%)
  waiting for transfers between devices  70 us (19%)
  starting transfers between devices  56.5 us (16%)
  between operations  14.1 us (4%)
  other arithmetic  13.2 us (4%)
  local copies, waits for them, and re-layouts  8.83 us (2%)
    pallas_call x8, Pallas kernels, shard_product(): pl.pallas_call(kernel, grid_spec=pltpu.PrefetchScalarGridSpec(num_scalar_...  184 us
    ppermute x10, starting transfers between devices, per_device(): sums[t][c].add(lax.ppermute(mine, 'row', pairs), pairs)  29.4 us
    ppermute x6, waiting for transfers between devices, spread_sites(): lax.ppermute(part, 'col', plan.site_pairs(m))  26.1 us
    ppermute x10, waiting for transfers between devices, per_device(): sums[t][c].add(lax.ppermute(mine, 'row', pairs), pairs)  14.8 us
    pallas_call x1, Pallas kernels, oscillate(): pl.pallas_call(functools.partial(step_kernel, tiles, len(arrived[0])), gr...  12 us
    ppermute x6, waiting for transfers between devices, gather_sites(): lax.ppermute(part, 'col', plan.site_pairs(m))  11.5 us
    ppermute x5, starting transfers between devices, exchange_rows(): lax.ppermute(part, 'row', pairs)  11 us
    ppermute x5, waiting for transfers between devices, exchange_rows(): lax.ppermute(part, 'row', pairs)  9.55 us
  transfers between devices with their start and end apart: 38, of which 16 were waited for; matrix products, arithmetic and copies ran while one was open for 3% of the time, Pallas kernels for 51%

profile of v4, /device:TPU:0, one launch (start us, length us, event | category | flops | bytes accessed | tf_op | source)
XLA Modules:
  0.0 358.8 jit_solution(16929688426771398456)
XLA Ops:
  8.6 4.0 %collective-permute-start = (f32[64,1536]{1,0:T(8,128)S(1)}, f32[64,1536]{1,0:T(8,128)S(1)}, u32[]{:S(2)}, u32[]{:S(2)}) collective-permute-start(f32[64,1536]{1,0:T(8,128)S(1)} %get-tuple-element.61), channel_id=1, source_target_pairs={{0,6},{1,7},{2,4},{3,5},{4,2},{5,3},{6,0},{7,1},{8,14},{9,15},{10,... | collective-permute-start | bytes 1179656 | tf_op jit(solution)/shard_map/ppermute | solution.py:238
  13.2 9.3 %collective-permute-done = f32[64,1536]{1,0:T(8,128)S(1)} collective-permute-done((f32[64,1536]{1,0:T(8,128)S(1)}, f32[64,1536]{1,0:T(8,128)S(1)}, u32[]{:S(2)}, u32[]{:S(2)}) %collective-permute-start) | collective-permute-done | bytes 393248 | tf_op jit(solution)/shard_map/ppermute | solution.py:238
  22.5 7.6 %collective-permute-done.2 = f32[64,1536]{1,0:T(8,128)S(1)} collective-permute-done((f32[64,1536]{1,0:T(8,128)S(1)}, f32[64,1536]{1,0:T(8,128)S(1)}, u32[]{:S(2)}, u32[]{:S(2)}) %collective-permute-start.2) | collective-permute-done | bytes 393248 | tf_op jit(solution)/shard_map/ppermute | solution.py:238
  35.0 3.6 %collective-permute-start.6 = (f32[64,1536]{1,0:T(8,128)}, f32[64,1536]{1,0:T(8,128)S(1)}, u32[]{:S(2)}, u32[]{:S(2)}) collective-permute-start(f32[64,1536]{1,0:T(8,128)} %get-tuple-element.62), channel_id=1, source_target_pairs={{0,24},{8,16},{16,8},{24,0},{1,25},{9,17},{17,9},{25,1},{2,26},{10... | collective-permute-start | bytes 1179656 | tf_op jit(solution)/shard_map/ppermute | solution.py:249
  42.1 6.0 %collective-permute-done.6.refs_0_ = f32[64,1536]{1,0:T(8,128)S(1)} collective-permute-done((f32[64,1536]{1,0:T(8,128)}, f32[64,1536]{1,0:T(8,128)S(1)}, u32[]{:S(2)}, u32[]{:S(2)}) %collective-permute-start.6) | collective-permute-done | bytes 393248 | tf_op jit(solution)/shard_map/ppermute | solution.py:249
  53.4 5.5 %collective-permute-done.3 = f32[64,1536]{1,0:T(8,128)} collective-permute-done((f32[64,1536]{1,0:T(8,128)}, f32[64,1536]{1,0:T(8,128)}, u32[]{:S(2)}, u32[]{:S(2)}) %collective-permute-start.3) | collective-permute-done | bytes 393248 | tf_op jit(solution)/shard_map/ppermute | solution.py:238
  63.7 4.9 %collective-permute-done.10.refs_2_ = f32[64,1536]{1,0:T(8,128)S(1)} collective-permute-done((f32[64,1536]{1,0:T(8,128)S(1)}, f32[64,1536]{1,0:T(8,128)S(1)}, u32[]{:S(2)}, u32[]{:S(2)}) %collective-permute-start.10) | collective-permute-done | bytes 393248 | tf_op jit(solution)/shard_map/ppermute | solution.py:258
  69.1 6.6 %collective-permute-done.14.refs_6_ = f32[64,1536]{1,0:T(8,128)S(1)} collective-permute-done((f32[64,1536]{1,0:T(8,128)S(1)}, f32[64,1536]{1,0:T(8,128)S(1)}, u32[]{:S(2)}, u32[]{:S(2)}) %collective-permute-start.14) | collective-permute-done | bytes 393248 | tf_op jit(solution)/shard_map/ppermute | solution.py:258
  77.0 4.1 %collective-permute-start.8 = (f32[64,3072]{1,0:T(8,128)}, f32[64,3072]{1,0:T(8,128)S(1)}, u32[]{:S(2)}, u32[]{:S(2)}) collective-permute-start(f32[64,3072]{1,0:T(8,128)} %get-tuple-element.27), channel_id=1, source_target_pairs={{0,8},{8,0},{16,24},{24,16},{1,9},{9,1},{17,25},{25,17},{2,10},{10... | collective-permute-start | bytes 2359304 | tf_op jit(solution)/shard_map/ppermute | solution.py:249
  86.6 14.9 %products.8.refs_9_ = f32[256,1536]{1,0:T(8,128)} custom-call(s32[6]{0:T(128)} %stack.27.offsets, f32[64,1536]{1,0:T(8,128)} %copy-done.3, f32[64,1536]{1,0:T(8,128)} %copy-done.7, f32[64,1536]{1,0:T(8,128)} %copy-done.4, f32[64,1536]{1,0:T(8,128)} %copy-done.8, f32[64,1536]{1,0:T(8,128)} %copy-done.5, f32[64,1536]{1,0:T(8,128)} %copy-done.9, ...), custom_call_target="tpu_custom_call" | custom-call | tf_op jit(solution)/shard_map/products/pallas_call | solution.py:143
  110.0 15.4 %products.9 = f32[256,1536]{1,0:T(8,128)} custom-call(s32[6]{0:T(128)} %stack.27.offsets, f32[64,1536]{1,0:T(8,128)} %collective-permute-done.7.refs_0_.refs_8_, f32[64,1536]{1,0:T(8,128)} %copy-done.14, f32[64,1536]{1,0:T(8,128)} %copy-done.11, f32[64,1536]{1,0:T(8,128)} %copy-done.15, f32[64,1536]{1,0:T(8,128)} %copy-done.12, f32[64,1536]{1,0:T(8,128)} %copy-done.16, ...), custom_call_target="tpu_custom_call" | custom-call | tf_op jit(solution)/shard_map/products/pallas_call | solution.py:143
  132.0 25.2 %products.10 = f32[256,1536]{1,0:T(8,128)} custom-call(s32[6]{0:T(128)} %stack.27.offsets, f32[64,1536]{1,0:T(8,128)} %copy-done.3, f32[64,1536]{1,0:T(8,128)} %copy-done.7, f32[64,1536]{1,0:T(8,128)} %copy-done.4, f32[64,1536]{1,0:T(8,128)} %copy-done.8, f32[64,1536]{1,0:T(8,128)} %copy-done.5, f32[64,1536]{1,0:T(8,128)} %copy-done.9, ...), custom_call_target="tpu_custom_call" | custom-call | tf_op jit(solution)/shard_map/products/pallas_call | solution.py:143
  159.6 7.0 %collective-permute-done.25.refs_0_ = f32[256,1536]{1,0:T(8,128)S(1)} collective-permute-done((f32[256,1536]{1,0:T(8,128)S(1)}, f32[256,1536]{1,0:T(8,128)S(1)}, u32[]{:S(2)}, u32[]{:S(2)}) %collective-permute-start.25) | collective-permute-done | bytes 1572896 | tf_op jit(solution)/shard_map/ppermute | solution.py:365
  166.6 6.7 %all-gather.9.cloned.1.call-done = f32[512,3072]{1,0:T(8,128)} async-done(((f32[64,3072]{1,0:T(8,128)}), f32[512,3072]{1,0:T(8,128)}) %all-gather.9.cloned.1.call-update) | async-done | bytes 6291472 | tf_op jit(solution)/shard_map/all_gather | solution.py:253
  173.3 22.4 %products.11 = f32[256,1536]{1,0:T(8,128)} custom-call(f32[4,2,64,3072]{3,2,1,0:T(8,128)} %bitcast.11, f32[6144,3072]{1,0:T(8,128)} %c_ref.4, f32[256,1536]{1,0:T(8,128)} %copy-done.21), custom_call_target="tpu_custom_call" | custom-call | tf_op jit(solution)/shard_map/products/pallas_call | solution.py:143
  195.7 4.6 %collective-permute-start.27 = (f32[256,1536]{1,0:T(8,128)}, f32[256,1536]{1,0:T(8,128)}, u32[]{:S(2)}, u32[]{:S(2)}) collective-permute-start(f32[256,1536]{1,0:T(8,128)} %products.11), channel_id=1, source_target_pairs={{0,8},{24,16},{1,9},{25,17},{2,10},{26,18},{3,11},{27,19},{4,12},{... | collective-permute-start | bytes 4718600 | tf_op jit(solution)/shard_map/ppermute | solution.py:365
  202.3 22.4 %products.12 = f32[256,1536]{1,0:T(8,128)} custom-call(f32[4,2,64,3072]{3,2,1,0:T(8,128)} %bitcast.12, f32[6144,3072]{1,0:T(8,128)} %c_ref.4, f32[256,1536]{1,0:T(8,128)} %collective-permute-done.26.refs_0_), custom_call_target="tpu_custom_call" | custom-call | tf_op jit(solution)/shard_map/products/pallas_call | solution.py:143
  228.4 5.9 %collective-permute-done.27 = f32[256,1536]{1,0:T(8,128)} collective-permute-done((f32[256,1536]{1,0:T(8,128)}, f32[256,1536]{1,0:T(8,128)}, u32[]{:S(2)}, u32[]{:S(2)}) %collective-permute-start.27) | collective-permute-done | bytes 1572896 | tf_op jit(solution)/shard_map/ppermute | solution.py:365
  234.2 22.5 %products.13 = f32[256,1536]{1,0:T(8,128)} custom-call(f32[4,2,64,3072]{3,2,1,0:T(8,128)} %bitcast.9, f32[6144,3072]{1,0:T(8,128)} %c_ref.4, f32[256,1536]{1,0:T(8,128)} %collective-permute-done.28.refs_0_), custom_call_target="tpu_custom_call" | custom-call | tf_op jit(solution)/shard_map/products/pallas_call | solution.py:143
  256.7 4.6 %collective-permute-start.32 = (f32[256,1536]{1,0:T(8,128)}, f32[256,1536]{1,0:T(8,128)}, u32[]{:S(2)}, u32[]{:S(2)}) collective-permute-start(f32[256,1536]{1,0:T(8,128)} %products.13), channel_id=1, source_target_pairs={{0,8},{24,16},{16,24},{8,0},{1,9},{25,17},{17,25},{9,1},{2,10},{26... | collective-permute-start | bytes 4718600 | tf_op jit(solution)/shard_map/ppermute | solution.py:365
  267.9 22.3 %products.14 = f32[256,1536]{1,0:T(8,128)} custom-call(f32[4,2,64,3072]{3,2,1,0:T(8,128)} %bitcast.10, f32[6144,3072]{1,0:T(8,128)} %c_ref.4, f32[256,1536]{1,0:T(8,128)} %collective-permute-done.30.refs_0_), custom_call_target="tpu_custom_call" | custom-call | tf_op jit(solution)/shard_map/products/pallas_call | solution.py:143
  292.3 6.5 %collective-permute-start.34 = (f32[256,1536]{1,0:T(8,128)}, f32[256,1536]{1,0:T(8,128)S(1)}, u32[]{:S(2)}, u32[]{:S(2)}) collective-permute-start(f32[256,1536]{1,0:T(8,128)} %products.14), channel_id=1, source_target_pairs={{0,8},{24,16},{16,24},{8,0},{1,9},{25,17},{17,25},{9,1},{2,10},{26... | collective-permute-start | bytes 4718600 | tf_op jit(solution)/shard_map/ppermute | solution.py:365
  298.8 39.1 %products.15.own_ref = f32[256,3072]{1,0:T(8,128)} custom-call(f32[4,2,64,3072]{3,2,1,0:T(8,128)} %bitcast.13, f32[6144,3072]{1,0:T(8,128)} %c_ref.4), custom_call_target="tpu_custom_call" | custom-call | tf_op jit(solution)/shard_map/products/pallas_call | solution.py:143
  340.3 12.0 %oscillate.1 = (f32[256,3072]{1,0:T(8,128)}, f32[256,3072]{1,0:T(8,128)}) custom-call(f32[256,3072]{1,0:T(8,128)} %x_ref.1, f32[256,3072]{1,0:T(8,128)} %y_ref.1, f32[256,3072]{1,0:T(8,128)} %products.15.own_ref, f32[256,1536]{1,0:T(8,128)} %collective-permute-done.31.refs_0_, f32[256,1536]{1,0:T(8,128)} %collective-permute-done.32.refs_1_, ...), custom_call_target="tpu_custom_call" | custom-call | tf_op jit(solution)/shard_map/oscillate/pallas_call | solution.py:109
  (121 shorter events, 61.8 us)
Async XLA Ops:
  7.2 166.2 %all-gather.9.cloned.1.call-start = ((), (), s32[]{:S(2)}) async-start(), calls=%async_computation.1 | async-start | bytes 7077888 | tf_op jit(solution)/shard_map/all_gather | solution.py:253
  40.2 18.7 %collective-permute-start.3 = (f32[64,1536]{1,0:T(8,128)}, f32[64,1536]{1,0:T(8,128)}, u32[]{:S(2)}, u32[]{:S(2)}) collective-permute-start(f32[64,1536]{1,0:T(8,128)} %get-tuple-element.57), channel_id=1, source_target_pairs={{0,4},{1,5},{2,6},{3,7},{4,0},{5,1},{6,2},{7,3},{8,12},{9,13},{10,... | collective-permute-start | bytes 1179656 | tf_op jit(solution)/shard_map/ppermute | solution.py:238
  41.5 18.7 %collective-permute-start.5 = (f32[64,1536]{1,0:T(8,128)}, f32[64,1536]{1,0:T(8,128)}, u32[]{:S(2)}, u32[]{:S(2)}) collective-permute-start(f32[64,1536]{1,0:T(8,128)} %get-tuple-element.56), channel_id=1, source_target_pairs={{0,2},{1,3},{2,0},{3,1},{4,6},{5,7},{6,4},{7,5},{8,10},{9,11},{10,... | collective-permute-start | bytes 1179656 | tf_op jit(solution)/shard_map/ppermute | solution.py:238
  48.1 20.5 %collective-permute-start.10 = (f32[64,1536]{1,0:T(8,128)S(1)}, f32[64,1536]{1,0:T(8,128)S(1)}, u32[]{:S(2)}, u32[]{:S(2)}) collective-permute-start(f32[64,1536]{1,0:T(8,128)S(1)} %collective-permute-done.6.refs_0_), channel_id=1, source_target_pairs={{0,2},{1,3},{2,0},{3,1},{4,6},{5,7},{6,4},{7,5},{8,10},{9,11},{10,... | collective-permute-start | bytes 1179656 | tf_op jit(solution)/shard_map/ppermute | solution.py:258
  49.6 19.0 %collective-permute-start.12 = (f32[64,1536]{1,0:T(8,128)S(1)}, f32[64,1536]{1,0:T(8,128)S(1)}, u32[]{:S(2)}, u32[]{:S(2)}) collective-permute-start(f32[64,1536]{1,0:T(8,128)S(1)} %collective-permute-done.6.refs_0_), channel_id=1, source_target_pairs={{0,4},{1,5},{2,6},{3,7},{4,0},{5,1},{6,2},{7,3},{8,12},{9,13},{10,... | collective-permute-start | bytes 1179656 | tf_op jit(solution)/shard_map/ppermute | solution.py:258
  51.8 23.9 %collective-permute-start.14 = (f32[64,1536]{1,0:T(8,128)S(1)}, f32[64,1536]{1,0:T(8,128)S(1)}, u32[]{:S(2)}, u32[]{:S(2)}) collective-permute-start(f32[64,1536]{1,0:T(8,128)S(1)} %collective-permute-done.6.refs_0_), channel_id=1, source_target_pairs={{0,6},{1,7},{2,4},{3,5},{4,2},{5,3},{6,0},{7,1},{8,14},{9,15},{10,... | collective-permute-start | bytes 1179656 | tf_op jit(solution)/shard_map/ppermute | solution.py:258
  77.0 28.7 %collective-permute-start.8 = (f32[64,3072]{1,0:T(8,128)}, f32[64,3072]{1,0:T(8,128)S(1)}, u32[]{:S(2)}, u32[]{:S(2)}) collective-permute-start(f32[64,3072]{1,0:T(8,128)} %get-tuple-element.27), channel_id=1, source_target_pairs={{0,8},{8,0},{16,24},{24,16},{1,9},{9,1},{17,25},{25,17},{2,10},{10... | collective-permute-start | bytes 2359304 | tf_op jit(solution)/shard_map/ppermute | solution.py:249
  81.1 20.5 %collective-permute-start.17 = (f32[64,1536]{1,0:T(8,128)}, f32[64,1536]{1,0:T(8,128)S(1)}, u32[]{:S(2)}, u32[]{:S(2)}) collective-permute-start(f32[64,1536]{1,0:T(8,128)} %collective-permute-done.7.refs_0_.refs_8_), channel_id=1, source_target_pairs={{0,2},{1,3},{2,0},{3,1},{4,6},{5,7},{6,4},{7,5},{8,10},{9,11},{10,... | collective-permute-start | bytes 1179656 | tf_op jit(solution)/shard_map/ppermute | solution.py:258
  82.7 18.9 %collective-permute-start.19 = (f32[64,1536]{1,0:T(8,128)}, f32[64,1536]{1,0:T(8,128)S(1)}, u32[]{:S(2)}, u32[]{:S(2)}) collective-permute-start(f32[64,1536]{1,0:T(8,128)} %collective-permute-done.7.refs_0_.refs_8_), channel_id=1, source_target_pairs={{0,4},{1,5},{2,6},{3,7},{4,0},{5,1},{6,2},{7,3},{8,12},{9,13},{10,... | collective-permute-start | bytes 1179656 | tf_op jit(solution)/shard_map/ppermute | solution.py:258
  82.9 19.3 %collective-permute-start.21 = (f32[64,1536]{1,0:T(8,128)}, f32[64,1536]{1,0:T(8,128)S(1)}, u32[]{:S(2)}, u32[]{:S(2)}) collective-permute-start(f32[64,1536]{1,0:T(8,128)} %collective-permute-done.7.refs_0_.refs_8_), channel_id=1, source_target_pairs={{0,6},{1,7},{2,4},{3,5},{4,2},{5,3},{6,0},{7,1},{8,14},{9,15},{10,... | collective-permute-start | bytes 1179656 | tf_op jit(solution)/shard_map/ppermute | solution.py:258
  85.4 19.3 %collective-permute-start.23 = (f32[64,1536]{1,0:T(8,128)}, f32[64,1536]{1,0:T(8,128)}, u32[]{:S(2)}, u32[]{:S(2)}) collective-permute-start(f32[64,1536]{1,0:T(8,128)} %get-tuple-element.33), channel_id=1, source_target_pairs={{0,16},{8,24},{16,0},{24,8},{1,17},{9,25},{17,1},{25,9},{2,18},{10... | collective-permute-start | bytes 1179656 | tf_op jit(solution)/shard_map/ppermute | solution.py:249
  105.7 20.8 %collective-permute-start.24 = (f32[64,1536]{1,0:T(8,128)}, f32[64,1536]{1,0:T(8,128)S(1)}, u32[]{:S(2)}, u32[]{:S(2)}) collective-permute-start(f32[64,1536]{1,0:T(8,128)} %get-tuple-element.37), channel_id=1, source_target_pairs={{0,16},{8,24},{16,0},{24,8},{1,17},{9,25},{17,1},{25,9},{2,18},{10... | collective-permute-start | bytes 1179656 | tf_op jit(solution)/shard_map/ppermute | solution.py:249
  127.5 106.7 %all-gather.11.cloned.1.call-start = ((), (), s32[]{:S(2)}) async-start(), calls=%async_computation.2 | async-start | bytes 7077888 | tf_op jit(solution)/shard_map/all_gather | solution.py:253
  128.3 170.5 %all-gather.7.cloned.1.call-start = ((), (), s32[]{:S(2)}) async-start(), calls=%async_computation | async-start | bytes 7077888 | tf_op jit(solution)/shard_map/all_gather | solution.py:253
  129.0 37.6 %collective-permute-start.25 = (f32[256,1536]{1,0:T(8,128)S(1)}, f32[256,1536]{1,0:T(8,128)S(1)}, u32[]{:S(2)}, u32[]{:S(2)}) collective-permute-start(f32[256,1536]{1,0:T(8,128)S(1)} %copy-done), channel_id=1, source_target_pairs={{0,8},{24,16},{1,9},{25,17},{2,10},{26,18},{3,11},{27,19},{4,12},{... | collective-permute-start | bytes 4718600 | tf_op jit(solution)/shard_map/ppermute | solution.py:365
  157.2 45.1 %collective-permute-start.26 = (f32[256,1536]{1,0:T(8,128)}, f32[256,1536]{1,0:T(8,128)}, u32[]{:S(2)}, u32[]{:S(2)}) collective-permute-start(f32[256,1536]{1,0:T(8,128)} %products.10), channel_id=1, source_target_pairs={{0,8},{24,16},{1,9},{25,17},{2,10},{26,18},{3,11},{27,19},{4,12},{... | collective-permute-start | bytes 4718600 | tf_op jit(solution)/shard_map/ppermute | solution.py:365
  195.7 38.5 %collective-permute-start.27 = (f32[256,1536]{1,0:T(8,128)}, f32[256,1536]{1,0:T(8,128)}, u32[]{:S(2)}, u32[]{:S(2)}) collective-permute-start(f32[256,1536]{1,0:T(8,128)} %products.11), channel_id=1, source_target_pairs={{0,8},{24,16},{1,9},{25,17},{2,10},{26,18},{3,11},{27,19},{4,12},{... | collective-permute-start | bytes 4718600 | tf_op jit(solution)/shard_map/ppermute | solution.py:365
  200.4 33.9 %collective-permute-start.28 = (f32[256,1536]{1,0:T(8,128)}, f32[256,1536]{1,0:T(8,128)}, u32[]{:S(2)}, u32[]{:S(2)}) collective-permute-start(f32[256,1536]{1,0:T(8,128)} %products.11), channel_id=1, source_target_pairs={{8,16},{16,8},{9,17},{17,9},{10,18},{18,10},{11,19},{19,11},{12,20... | collective-permute-start | bytes 4718600 | tf_op jit(solution)/shard_map/ppermute | solution.py:365
  224.7 43.3 %collective-permute-start.29 = (f32[256,1536]{1,0:T(8,128)}, f32[256,1536]{1,0:T(8,128)S(1)}, u32[]{:S(2)}, u32[]{:S(2)}) collective-permute-start(f32[256,1536]{1,0:T(8,128)} %products.12), channel_id=1, source_target_pairs={{0,8},{24,16},{1,9},{25,17},{2,10},{26,18},{3,11},{27,19},{4,12},{... | collective-permute-start | bytes 4718600 | tf_op jit(solution)/shard_map/ppermute | solution.py:365
  226.5 41.4 %collective-permute-start.30 = (f32[256,1536]{1,0:T(8,128)}, f32[256,1536]{1,0:T(8,128)}, u32[]{:S(2)}, u32[]{:S(2)}) collective-permute-start(f32[256,1536]{1,0:T(8,128)} %products.12), channel_id=1, source_target_pairs={{8,16},{16,8},{9,17},{17,9},{10,18},{18,10},{11,19},{19,11},{12,20... | collective-permute-start | bytes 4718600 | tf_op jit(solution)/shard_map/ppermute | solution.py:365
  256.7 81.2 %collective-permute-start.32 = (f32[256,1536]{1,0:T(8,128)}, f32[256,1536]{1,0:T(8,128)}, u32[]{:S(2)}, u32[]{:S(2)}) collective-permute-start(f32[256,1536]{1,0:T(8,128)} %products.13), channel_id=1, source_target_pairs={{0,8},{24,16},{16,24},{8,0},{1,9},{25,17},{17,25},{9,1},{2,10},{26... | collective-permute-start | bytes 4718600 | tf_op jit(solution)/shard_map/ppermute | solution.py:365
  264.0 73.8 %collective-permute-start.31 = (f32[256,1536]{1,0:T(8,128)}, f32[256,1536]{1,0:T(8,128)}, u32[]{:S(2)}, u32[]{:S(2)}) collective-permute-start(f32[256,1536]{1,0:T(8,128)} %add.38), channel_id=1, source_target_pairs={{8,16},{16,8},{9,17},{17,9},{10,18},{18,10},{11,19},{19,11},{12,20... | collective-permute-start | bytes 4718600 | tf_op jit(solution)/shard_map/ppermute | solution.py:365
  291.6 46.3 %collective-permute-start.33 = (f32[256,1536]{1,0:T(8,128)}, f32[256,1536]{1,0:T(8,128)S(1)}, u32[]{:S(2)}, u32[]{:S(2)}) collective-permute-start(f32[256,1536]{1,0:T(8,128)} %add.39), channel_id=1, source_target_pairs={{8,16},{16,8},{9,17},{17,9},{10,18},{18,10},{11,19},{19,11},{12,20... | collective-permute-start | bytes 4718600 | tf_op jit(solution)/shard_map/ppermute | solution.py:365
  292.3 45.6 %collective-permute-start.34 = (f32[256,1536]{1,0:T(8,128)}, f32[256,1536]{1,0:T(8,128)S(1)}, u32[]{:S(2)}, u32[]{:S(2)}) collective-permute-start(f32[256,1536]{1,0:T(8,128)} %products.14), channel_id=1, source_target_pairs={{0,8},{24,16},{16,24},{8,0},{1,9},{25,17},{17,25},{9,1},{2,10},{26... | collective-permute-start | bytes 4718600 | tf_op jit(solution)/shard_map/ppermute | solution.py:365
  (37 other events, 292.0 us)
Sparse Core Ops, SparseCore 0:
  127.6 45.6 all-gather.8
  175.2 45.5 all-gather.10
  222.6 45.5 all-gather.6
